TPU v7x, 32 devices: a whole 2x2x4 slice. The times are simulated.
32 devices in a mesh: ctx: 8 (over z, x), ch: 2 (over y), dp: 2 (over core).
Axes of the slice: x: 2, y: 2, z: 4, core: 2. Of those that a mesh axis runs over, the one named last changes fastest.
Arguments:
- raw_streams: bfloat16 [16384, 3, 256], P(('dp', 'ctx'), None, 'ch'), parts along dimension 0, may hold values from -6 to 6
- short_taps: float32 [7, 3, 256], P(None, None, 'ch'), may hold values from -2.4 to 2.4
- decay_rate: float32 [16, 16], P('ch'), may hold values from 1.2207031e-06 to 0.08
- residue: float32 [16, 16], P('ch'), may hold values from -2 to 2
- medium_filter: float32 [16, 128], P('ch'), may hold values from -0.5 to 0.5
- cotangent: bfloat16 [16384, 256], P(('dp', 'ctx'), 'ch'), parts along dimension 0, may hold values from -6 to 6
Outputs:
- mixed_out: bfloat16 [16384, 256], P(('dp', 'ctx'), 'ch'), parts along dimension 0
- grad_streams: bfloat16 [16384, 3, 256], P(('dp', 'ctx'), None, 'ch'), parts along dimension 0
- grad_residue: float32 [32, 16], P(('dp', 'ch')), parts along dimension 0
There are 2 independent parts, one for each index of `dp`. A program takes and returns all parts, laid end to end along the dimension named above; an argument that names none is the same for every part. Nothing has to cross between parts.
All inputs are finite; a program needn't handle non-finite values.
Results may differ from a plain program's by a relative error of at most 0.002.
Values may be sent and summed in bfloat16 or wider, within the bound.
A program may use at most 64 MiB of HBM per device.

v0:
```python
import math

import jax
import jax.numpy as jnp
from jax import lax
from jax.sharding import PartitionSpec as P

BLOCK = 128


def shifted(block, axis, distance):
    devices = range(lax.axis_size(axis))
    route = [(i - distance, i) for i in devices if i - distance in devices]
    return lax.ppermute(block, axis, route)


def einsum_high(form, *operands):
    return jnp.einsum(form, *operands, precision=lax.Precision.HIGHEST)


def mode_stack(rate, block):
    positions = jnp.arange(block, dtype=jnp.int32)
    lagged = positions[:, None] - positions[None, :]
    lag_float = jnp.maximum(lagged, 0).astype(jnp.float32)
    return jnp.where(
        lagged[None, None] >= 0, jnp.exp(-rate[:, :, None, None] * lag_float[None, None]), 0.0
    )


def toeplitz_band(vector, block):
    groups, taps = vector.shape
    width = block + taps - 1
    padded = jnp.concatenate([vector, jnp.zeros((groups, width + 1 - taps), jnp.float32)], axis=1)
    tiled = jnp.tile(padded, (1, block))[:, : block * width]
    return tiled.reshape(groups, block, width)


def make_tables(rate, residue, medium, block):
    taps = medium.shape[1]
    scaled = jnp.sqrt(-jnp.expm1(-2.0 * rate))
    rhat = residue * scaled
    positions = jnp.arange(block, dtype=jnp.int32).astype(jnp.float32)
    after = jnp.exp(-rate[:, None, :] * (positions[None, :, None] + 1.0))
    into = jnp.exp(-rate[:, :, None] * (block - 1.0 - positions)[None, None, :])
    from_start = jnp.exp(-rate[:, :, None] * positions[None, None, :])
    to_end = rhat[:, None, :] * jnp.exp(-rate[:, None, :] * (block - positions)[None, :, None])
    whole = jnp.exp(-rate * float(block))
    stacked = mode_stack(rate, block)
    kernel = einsum_high("gm,gmts->gts", rhat, stacked)
    fwd_band = toeplitz_band(medium[:, ::-1], block)
    bwd_band = toeplitz_band(medium, block)
    fwd_prev = fwd_band[:, :, : taps - 1]
    fwd_join = kernel + fwd_band[:, :, taps - 1 :]
    bwd_join = jnp.swapaxes(kernel, 1, 2) + bwd_band[:, :, :block]
    bwd_next = bwd_band[:, :, block:]
    return (
        rhat,
        after,
        into,
        from_start,
        to_end,
        whole,
        fwd_join,
        fwd_prev,
        bwd_join,
        bwd_next,
        stacked,
    )


def forward_blocks(product, head, state_init, tables, block):
    (
        rhat,
        after,
        into,
        from_start,
        to_end,
        whole,
        fwd_join,
        fwd_prev,
        bwd_join,
        bwd_next,
        stacked,
    ) = tables
    lifted = rhat[:, None, :] * after
    rim = head.shape[0]
    count = product.shape[0] // block
    pieces = product.reshape((count, block) + product.shape[1:])
    prevs = jnp.concatenate([head[None], pieces[:-1, block - rim :]], axis=0)

    def forward_step(state, pair):
        piece, prev = pair
        mixed = einsum_high("gts,sgc->tgc", fwd_join, piece) + einsum_high(
            "gtm,gcm->tgc", lifted, state
        )
        mixed = mixed + einsum_high("gts,sgc->tgc", fwd_prev, prev)
        renewed = whole[:, None, :] * state + einsum_high("gms,sgc->gcm", into, piece)
        return (renewed, (mixed, state))

    _, (outputs, starts) = lax.scan(forward_step, state_init, (pieces, prevs))
    return (outputs.reshape(product.shape), starts)


def backward_blocks(grad_mixed, grad_tail, product, starts, carry_init, tables, block, rate):
    (
        rhat,
        after,
        into,
        from_start,
        to_end,
        whole,
        fwd_join,
        fwd_prev,
        bwd_join,
        bwd_next,
        stacked,
    ) = tables
    rim = grad_tail.shape[0]
    count = product.shape[0] // block
    grad_pieces = grad_mixed.reshape((count, block) + grad_mixed.shape[1:])
    pieces = product.reshape((count, block) + product.shape[1:])
    nexts = jnp.concatenate([grad_pieces[1:, :rim], grad_tail[None]], axis=0)

    def backward_step(carry, items):
        grad_state, running = carry
        grad_piece, following, piece, state = items
        grad_prod = einsum_high("gst,tgc->sgc", bwd_join, grad_piece) + einsum_high(
            "gsm,gcm->sgc", to_end, grad_state
        )
        grad_prod = grad_prod + einsum_high("gst,tgc->sgc", bwd_next, following)
        renewed = whole[:, None, :] * grad_state + einsum_high(
            "gmt,tgc->gcm", from_start, grad_piece
        )
        cross = einsum_high("tgc,sgc->gts", grad_piece, piece)
        inner = einsum_high("gts,gmts->gm", cross, stacked)
        running = running + inner + einsum_high("gtm,gcm,tgc->gm", after, state, grad_piece)
        return ((renewed, running), grad_prod)

    zero_total = jnp.zeros(rate.shape, jnp.float32)
    (_, running), grads = lax.scan(
        backward_step, (carry_init, zero_total), (grad_pieces, nexts, pieces, starts), reverse=True
    )
    return (grads.reshape(product.shape), running)


def short_filter(extended, weights, rows):
    short = weights.shape[0]
    total = weights[0] * extended[short - 1 : short - 1 + rows]
    for shift_by in range(1, short):
        total = (
            total + weights[shift_by] * extended[short - 1 - shift_by : short - 1 - shift_by + rows]
        )
    return total


def short_adjoint(extended, weights, rows):
    total = weights[0] * extended[0:rows]
    for shift_by in range(1, weights.shape[0]):
        total = total + weights[shift_by] * extended[shift_by : shift_by + rows]
    return total


def device_weights(decay_rate, distance, rows):
    steps_float = (jnp.maximum(distance, 0) * rows).astype(jnp.float32)
    return jnp.where(
        distance[:, None, None] >= 0, jnp.exp(-decay_rate[None] * steps_float[:, None, None]), 0.0
    )


def body(raw_streams, short_taps, decay_rate, residue, medium_filter, cotangent):
    rows = raw_streams.shape[0]
    chans = raw_streams.shape[2]
    groups, modes = decay_rate.shape
    per_group = chans // groups
    short = short_taps.shape[0]
    taps = medium_filter.shape[1]
    my_index = lax.axis_index("ctx")
    ctx_count = lax.axis_size("ctx")
    head_rows = shifted(raw_streams[rows - (short - 1) :], "ctx", 1)
    extended = jnp.concatenate([head_rows, raw_streams]).astype(jnp.float32)
    featured = short_filter(extended, short_taps, rows)
    flat_product = featured[:, 1] * featured[:, 2]
    product_head = shifted(flat_product[rows - (taps - 1) :].astype(jnp.bfloat16), "ctx", 1).astype(
        jnp.float32
    )
    query = featured[:, 0]
    keys = featured[:, 1]
    values = featured[:, 2]
    product = flat_product.reshape(rows, groups, per_group)
    head = product_head.reshape(taps - 1, groups, per_group)
    grad_out = cotangent.astype(jnp.float32)
    grad_flat = grad_out * query
    grad_mixed = grad_flat.reshape(rows, groups, per_group)
    grad_tail = shifted(grad_flat[: taps - 1].astype(jnp.bfloat16), "ctx", -1).astype(jnp.float32)
    tail = grad_tail.reshape(taps - 1, groups, per_group)
    positions = jnp.arange(rows, dtype=jnp.int32).astype(jnp.float32)
    into_device = jnp.exp(-decay_rate[:, :, None] * (rows - 1.0 - positions)[None, None, :])
    from_device = jnp.exp(-decay_rate[:, :, None] * positions[None, None, :])
    final_state = einsum_high("gms,sgc->gcm", into_device, product)
    first_grad = einsum_high("gmt,tgc->gcm", from_device, grad_mixed)
    zero_state = jnp.zeros((groups, per_group, modes), jnp.float32)
    paired = jnp.stack([final_state, first_grad])[None]
    total = jnp.stack([zero_state, zero_state])
    piece = lax.all_gather(paired, "ctx", axis=0, tiled=True)
    device = jnp.arange(piece.shape[0], dtype=jnp.int32)
    lower = device_weights(decay_rate, my_index - 1 - device, rows)
    higher = device_weights(decay_rate, device - my_index - 1, rows)
    forward_part = total[0] + einsum_high("ngm,ngcm->gcm", lower, piece[:, 0])
    backward_part = total[1] + einsum_high("ngm,ngcm->gcm", higher, piece[:, 1])
    both = jnp.stack([forward_part, backward_part])
    carry_in = both[0]
    grad_carry = both[1]
    tables = make_tables(decay_rate, residue, medium_filter, BLOCK)
    mixed, starts = forward_blocks(product, head, carry_in, tables, BLOCK)
    mixed = mixed.reshape(rows, chans)
    mixed_out = (query * mixed).astype(jnp.bfloat16)
    grad_query = grad_out * mixed
    grad_prod, running = backward_blocks(
        grad_mixed, tail, product, starts, grad_carry, tables, BLOCK, decay_rate
    )
    grad_prod = grad_prod.reshape(rows, chans)
    grad_featured = jnp.stack([grad_query, grad_prod * values, grad_prod * keys], axis=1)
    featured_tail = shifted(grad_featured[: short - 1], "ctx", -1)
    grad_padded = jnp.concatenate([grad_featured, featured_tail])
    grad_streams = short_adjoint(grad_padded, short_taps, rows).astype(jnp.bfloat16)
    summed = lax.psum(running, "ctx")
    scaled = jnp.sqrt(-jnp.expm1(-2.0 * decay_rate))
    grad_residue = summed * scaled / math.sqrt(float(rows * ctx_count * per_group))
    return (mixed_out, grad_streams, grad_residue)


def solution(mesh):
    in_specs = (
        P(("dp", "ctx"), None, "ch"),
        P(None, None, "ch"),
        P("ch", None),
        P("ch", None),
        P("ch", None),
        P(("dp", "ctx"), "ch"),
    )
    out_specs = (P(("dp", "ctx"), "ch"), P(("dp", "ctx"), None, "ch"), P(("dp", "ch"), None))
    return jax.shard_map(body, mesh=mesh, in_specs=in_specs, out_specs=out_specs, check_vma=False)
```

profile of v0, /device:TPU:0, one launch (start us, length us, event | category | flops | bytes accessed | tf_op | source)
XLA Modules:
  0.0 284.6 jit_solution(2099710338804304164)
XLA Ops:
  1.5 5.5 %collective-permute-start = (bf16[6,3,128]{0,2,1:T(8,128)(2,1)S(1)}, bf16[6,3,128]{0,2,1:T(8,128)(2,1)}, u32[]{:S(2)}, u32[]{:S(2)}) collective-permute-start(bf16[6,3,128]{0,2,1:T(8,128)(2,1)S(1)} %copy.38), channel_id=1, source_target_pairs={{0,4},{4,8},{8,12},{12,16},{16,20},{20,24},{24,28},{1,5},{5,9},{9,... | collective-permute-start | bytes 13832 | tf_op jit(solution)/shard_map/ppermute | solution.py:14
  12.7 7.7 %fusion.51 = f32[8,1,128,128]{3,1,2,0:T(1,128)S(1)} fusion(f32[8,16,1,1]{1,2,3,0:T(1,128)S(1)} %bitcast.223, f32[8,16,128,128]{3,2,1,0:T(8,128)S(1)} %exponential_select_fusion), kind=kOutput, calls=%fused_computation.57 | convolution fusion | flops 25165824 | bytes 8913408 | tf_op jit(solution)/shard_map/gm,gmts->gts/dot_general | solution.py:18
  30.1 3.2 %fusion.60 = f32[1024,3,128]{0,2,1:T(8,128)S(1)} fusion(f32[1030,3,128]{0,2,1:T(8,128)S(1)} %maximum_convert_fusion, f32[3,128]{1,0:T(4,128)S(1)} %get-tuple-element.772, f32[3,128]{1,0:T(4,128)S(1)} %get-tuple-element.773, f32[3,128]{1,0:T(4,128)S(1)} %get-tuple-element.774, f32[3,128]{1,0:T(4,128)S(1)} %get-tuple-element.775, ...), kind=kLoop, calls=%fused_computation.75 | loop fusion | flops 5111808 | bytes 12593664 | tf_op jit(solution)/shard_map/add | solution.py:151
  33.5 3.0 %collective-permute-start.1 = (bf16[127,128]{0,1:T(8,128)(2,1)S(1)}, bf16[127,128]{0,1:T(8,128)(2,1)S(1)}, u32[]{:S(2)}, u32[]{:S(2)}) collective-permute-start(bf16[127,128]{0,1:T(8,128)(2,1)S(1)} %fusion.81), channel_id=1, source_target_pairs={{0,4},{4,8},{8,12},{12,16},{16,20},{20,24},{24,28},{1,5},{5,9},{9,... | collective-permute-start | bytes 97544 | tf_op jit(solution)/shard_map/ppermute | solution.py:14
  39.0 32.9 %all-gather = f32[16,8,16,16]{3,2,1,0:T(8,128)S(1)} all-gather(f32[2,8,16,16]{3,2,1,0:T(8,128)S(1)} %pad_maximum_fusion.4), channel_id=2, replica_groups=mesh['ctx'=8,'ch'=2,'dp'=2] {'ctx'}, dimensions={0}, use_global_device_ids=true | all-gather | bytes 147456 | tf_op jit(solution)/shard_map/all_gather | solution.py:204
  79.2 69.3 %while.37 = (s32[]{:T(128)}, f32[8,16,16]{2,1,0:T(8,128)S(1)}, f32[8,128,8,16]{1,0,3,2:T(8,128)}, f32[8,8,16,16]{3,2,1,0:T(8,128)}, f32[8,16]{1,0:T(8,128)S(1)},...) while((s32[]{:T(128)}, f32[8,16,16]{2,1,0:T(8,128)S(1)}, ...), condition=%wide.region_1.2_spmd.clone.clone, body=%wide.region_0.1_spmd.clone.clone.sunk | while | flops 56512512 | bytes 1932437 | solution.py:100
  83.2 2.8 dynamic_update_slice.29
  91.9 2.8 dynamic_update_slice.29
  100.6 2.8 dynamic_update_slice.29
  109.2 2.8 dynamic_update_slice.29
  117.9 2.8 dynamic_update_slice.29
  126.6 2.8 dynamic_update_slice.29
  135.2 2.8 dynamic_update_slice.29
  151.5 101.7 %while.38 = (s32[]{:T(128)}, f32[8,16,16]{2,1,0:T(8,128)S(1)}, f32[8,16]{1,0:T(8,128)S(1)}, f32[8,128,8,16]{1,0,3,2:T(8,128)}, f32[8,16]{1,0:T(8,128)S(1)}, /*in...) while((s32[]{:T(128)}, f32[8,16,16]{2,1,0:T(8,128)S(1)}, ...), condition=%wide.region_3.4_spmd.clone.clone.clone, body=%wide.region_2.3_spmd.clone.clone.clone.sunk | while | flops 93233280 | bytes 3328231 | solution.py:140
  161.0 2.8 dynamic_update_slice.30
  173.8 2.8 dynamic_update_slice.30
  186.5 2.8 dynamic_update_slice.30
  199.2 2.8 dynamic_update_slice.30
  211.9 2.8 dynamic_update_slice.30
  224.6 2.8 dynamic_update_slice.30
  237.4 2.8 dynamic_update_slice.30
  250.1 2.8 dynamic_update_slice.30
  257.2 20.9 %psum.7 = f32[8,16]{1,0:T(8,128)S(1)} all-reduce(f32[8,16]{1,0:T(8,128)S(1)} %get-tuple-element.358), channel_id=1, replica_groups=mesh['ctx'=8,'ch'=2,'dp'=2] {'ctx'}, use_global_device_ids=true, to_apply=%region_4.5 | all-reduce | flops 128 | bytes 1024 | tf_op jit(solution)/shard_map/psum | solution.py:226
  280.2 3.2 %fusion.54 = bf16[1024,3,128]{0,2,1:T(8,128)(2,1)S(1)} fusion(f32[1030,3,128]{0,2,1:T(8,128)S(1)} %pad_maximum_fusion, f32[3,128]{1,0:T(4,128)S(1)} %get-tuple-element.772, f32[3,128]{1,0:T(4,128)S(1)} %get-tuple-element.773, f32[3,128]{1,0:T(4,128)S(1)} %get-tuple-element.774, f32[3,128]{1,0:T(4,128)S(1)} %copy-done.9, f32[3,128]{1,0:T(4,128)S(1)} %copy-done.11, ...), kind=kLoop, calls=%fused_computation.63 | loop fusion | flops 6291456 | bytes 11807232 | tf_op jit(solution)/shard_map/convert_element_type | solution.py:225
  (252 shorter events, 164.1 us)
Async XLA Ops:
  1.5 27.3 %collective-permute-start = (bf16[6,3,128]{0,2,1:T(8,128)(2,1)S(1)}, bf16[6,3,128]{0,2,1:T(8,128)(2,1)}, u32[]{:S(2)}, u32[]{:S(2)}) collective-permute-start(bf16[6,3,128]{0,2,1:T(8,128)(2,1)S(1)} %copy.38), channel_id=1, source_target_pairs={{0,4},{4,8},{8,12},{12,16},{16,20},{20,24},{24,28},{1,5},{5,9},{9,... | collective-permute-start | bytes 13832 | tf_op jit(solution)/shard_map/ppermute | solution.py:14
  10.0 1.5 copy-start.16
  10.0 1.5 copy-start.22
  11.5 11.3 %copy-start.1 = (f32[8,128,255]{2,1,0:T(8,128)}, f32[8,128,255]{2,1,0:T(8,128)S(1)}, u32[]{:S(2)}) copy-start(f32[8,128,255]{2,1,0:T(8,128)S(1)} %reshape.118) | copy-start | bytes 3133444
  11.5 18.5 %copy-start.8 = (f32[3,128]{1,0:T(4,128)}, f32[3,128]{1,0:T(4,128)S(1)}, u32[]{:S(2)}) copy-start(f32[3,128]{1,0:T(4,128)S(1)} %get-tuple-element.775) | copy-start | bytes 4612
  11.5 18.5 %copy-start.10 = (f32[3,128]{1,0:T(4,128)}, f32[3,128]{1,0:T(4,128)S(1)}, u32[]{:S(2)}) copy-start(f32[3,128]{1,0:T(4,128)S(1)} %get-tuple-element.776) | copy-start | bytes 4612
  11.5 18.5 %copy-start.12 = (f32[3,128]{1,0:T(4,128)}, f32[3,128]{1,0:T(4,128)S(1)}, u32[]{:S(2)}) copy-start(f32[3,128]{1,0:T(4,128)S(1)} %get-tuple-element.777) | copy-start | bytes 4612
  20.5 1.1 copy-start.6
  20.7 2.1 copy-start.18
  24.4 3.0 %copy-start = (f32[8,128,255]{2,1,0:T(8,128)}, f32[8,128,255]{2,1,0:T(8,128)S(1)}, u32[]{:S(2)}) copy-start(f32[8,128,255]{2,1,0:T(8,128)S(1)} %reshape.119) | copy-start | bytes 3133444
  24.4 1.1 copy-start.7
  25.5 4.5 %copy-start.14 = (f32[1,3,128]{2,1,0:T(4,128)}, f32[1,3,128]{2,1,0:T(4,128)S(1)}, u32[]{:S(2)}) copy-start(f32[1,3,128]{2,1,0:T(4,128)S(1)} %copy.118) | copy-start | bytes 4612
  27.4 1.4 copy-start.2
  33.3 3.2 %copy-start.3 = (bf16[1024,128]{0,1:T(8,128)(2,1)S(1)}, bf16[1024,128]{0,1:T(8,128)(2,1)}, u32[]{:S(2)}) copy-start(bf16[1024,128]{0,1:T(8,128)(2,1)} %copy.40) | copy-start | bytes 786436
  33.5 43.9 %collective-permute-start.1 = (bf16[127,128]{0,1:T(8,128)(2,1)S(1)}, bf16[127,128]{0,1:T(8,128)(2,1)S(1)}, u32[]{:S(2)}, u32[]{:S(2)}) collective-permute-start(bf16[127,128]{0,1:T(8,128)(2,1)S(1)} %fusion.81), channel_id=1, source_target_pairs={{0,4},{4,8},{8,12},{12,16},{16,20},{20,24},{24,28},{1,5},{5,9},{9,... | collective-permute-start | bytes 97544 | tf_op jit(solution)/shard_map/ppermute | solution.py:14
  74.7 73.8 %collective-permute-start.2 = (bf16[127,128]{0,1:T(8,128)(2,1)}, bf16[127,128]{0,1:T(8,128)(2,1)S(1)}, u32[]{:S(2)}, u32[]{:S(2)}) collective-permute-start(bf16[127,128]{0,1:T(8,128)(2,1)} %slice.274), channel_id=1, source_target_pairs={{4,0},{8,4},{12,8},{16,12},{20,16},{24,20},{28,24},{5,1},{9,5},{13... | collective-permute-start | bytes 97544 | tf_op jit(solution)/shard_map/ppermute | solution.py:14
  76.5 2.7 slice-start.1
  76.5 2.7 copy-start.21
  148.5 2.9 %slice-start = ((f32[8,128,255]{2,1,0:T(8,128)}), f32[8,128,127]{2,1,0:T(8,128)S(1)}, s32[]{:S(2)}) async-start(f32[8,128,255]{2,1,0:T(8,128)} %copy-done), calls=%async_computation | async-start | bytes 1048576 | tf_op jit(solution)/shard_map/slice | solution.py:55
  148.5 2.9 %copy-start.19 = (f32[128]{0:T(128)S(1)}, f32[128]{0:T(128)}, u32[]{:S(2)}) copy-start(f32[128]{0:T(128)} %broadcast_subtract_fusion.1) | copy-start | bytes 1540
  148.5 2.9 %copy-start.20 = (f32[128]{0:T(128)S(1)}, f32[128]{0:T(128)}, u32[]{:S(2)}) copy-start(f32[128]{0:T(128)} %iota_convert_fusion.1) | copy-start | bytes 1540
  254.3 1.1 copy-start.5
  255.6 22.4 %copy-start.17 = (f32[8,16]{1,0:T(8,128)S(1)}, f32[8,16]{1,0:T(8,128)}, u32[]{:S(2)}) copy-start(f32[8,16]{1,0:T(8,128)} %param.12) | copy-start | bytes 1540
  255.9 23.6 %collective-permute-start.3 = (f32[6,3,128]{0,2,1:T(8,128)S(1)}, f32[6,3,128]{0,2,1:T(8,128)S(1)}, u32[]{:S(2)}, u32[]{:S(2)}) collective-permute-start(f32[6,3,128]{0,2,1:T(8,128)S(1)} %slice.182), channel_id=1, source_target_pairs={{4,0},{8,4},{12,8},{16,12},{20,16},{24,20},{28,24},{5,1},{9,5},{13... | collective-permute-start | bytes 27656 | tf_op jit(solution)/shard_map/ppermute | solution.py:14
  (5 other events, 3.7 us)
where the time goes:
time: 288 us; the launch traced here: 285 us
  local copies, waits for them, and re-layouts  97.7 us (34%)
  matrix products  85.4 us (30%)
  blocking collectives  53.8 us (19%)
  other arithmetic  34.6 us (12%)
  starting transfers between devices  11.1 us (4%)
    dot_general x83, matrix products, einsum_high(): return jnp.einsum(form, *operands, precision=lax.Precision.HIGHEST)  85.4 us
    dynamic_update_slice x24, local copies, waits for them, and re-layouts, forward_blocks(): _, (outputs, starts) = lax.scan(forward_step, state_init, (pieces, prevs))  49.9 us
    all_gather x1, blocking collectives, body(): piece = lax.all_gather(paired, 'ctx', axis=0, tiled=True)  32.9 us
    dynamic_slice x24, local copies, waits for them, and re-layouts, forward_blocks(): _, (outputs, starts) = lax.scan(forward_step, state_init, (pieces, prevs))  26.5 us
    psum x1, blocking collectives, body(): summed = lax.psum(running, 'ctx')  20.9 us
    dot_general x9, other arithmetic, einsum_high(): return jnp.einsum(form, *operands, precision=lax.Precision.HIGHEST)  18.1 us
    ppermute x4, starting transfers between devices, shifted(): return lax.ppermute(block, axis, route)  11.1 us
    unnamed x59, local copies, waits for them, and re-layouts  9.97 us
  transfers between devices with their start and end apart: 4, of which 0 were waited for; matrix products, arithmetic and copies ran while one was open for 35% of the time, Pallas kernels for 0%

commit v1 on v0

v1 whole, which is shorter than its diff:
```python
import functools
import math

import jax
import jax.numpy as jnp
from jax import lax
from jax.experimental import pallas as pl
from jax.experimental.pallas import tpu as pltpu
from jax.sharding import PartitionSpec as P

F32 = jnp.float32
BF16 = jnp.bfloat16
MESH = pl.DeviceIdType.MESH
B = 128
HIGH = lax.Precision.HIGHEST


def dot(a, b, ca, cb):
    return lax.dot_general(
        a, b, (((ca,), (cb,)), ((), ())), precision=HIGH, preferred_element_type=F32
    )


def lanes(shape):
    return lax.broadcasted_iota(jnp.int32, shape, 1)


def rolled(x, shift):
    shift = shift % x.shape[1]
    return pltpu.roll(x, shift, 1) if shift else x


def block_transpose(xs, width):
    count = len(xs)
    chunk = lanes(xs[0].shape) // width
    xs = list(xs)
    bit = 1
    while bit < count:
        high = (chunk & bit) != 0
        for i in range(count):
            if i & bit == 0:
                a, d = xs[i], xs[i | bit]
                xs[i] = jnp.where(high, rolled(d, width * bit), a)
                xs[i | bit] = jnp.where(high, d, rolled(a, -width * bit))
        bit *= 2
    return xs


def kernel(
    n, groups, modes,
    raw, taps, cot, rate_ref, rhat_ref, ratec_ref, w_ref,
    mixed_out, grad_out, res_out,
    hkv, hq, nq, ncot, ext, feat, hext, qext, yp, yg, head, tail,
    s_all, u_all, msg1, msg2, got1, got2, of, ob, gf, gfr,
    hs, hr, m1s, m1r, m2s, m2r, gs, gr,
):
    rows, chans = cot.shape
    per = chans // groups
    count = rows // B
    short = taps.shape[1]
    me = lax.axis_index("ctx")
    nxt = lax.rem(me + 1, n)
    prv = lax.rem(me + n - 1, n)
    barrier = pltpu.get_barrier_semaphore()
    for k in range(1, n):
        pl.semaphore_signal(
            barrier, inc=1, device_id={"ctx": lax.rem(me + k, n)}, device_id_type=MESH
        )
    pl.semaphore_wait(barrier, n - 1)

    def send(src, dst, ssem, rsem, to):
        copy = pltpu.make_async_remote_copy(
            src_ref=src, dst_ref=dst, send_sem=ssem, recv_sem=rsem,
            device_id={"ctx": to}, device_id_type=MESH,
        )
        copy.start()
        return copy

    halo = [
        send(raw.at[0:1, rows - 16 : rows], hq, hs.at[0], hr.at[0], nxt),
        send(raw.at[1:3, rows - 144 : rows], hkv, hs.at[1], hr.at[1], nxt),
        send(raw.at[0:1, 0:B], nq, hs.at[2], hr.at[2], prv),
        send(cot.at[0:B], ncot, hs.at[3], hr.at[3], prv),
    ]

    has_prev = jnp.where(me > 0, 1.0, 0.0).astype(F32)
    has_next = jnp.where(me < n - 1, 1.0, 0.0).astype(F32)
    tap = [[taps[i, k : k + 1, :] for k in range(short)] for i in range(3)]

    def filtered(ref, i, slot, start, size):
        total = tap[i][0] * ref[slot, start : start + size, :]
        for k in range(1, short):
            total = total + tap[i][k] * ref[slot, start - k : start - k + size, :]
        return total

    for j in range(count):
        for i in range(3):
            ext[i, 8 + j * B : 8 + (j + 1) * B, :] = raw[i, j * B : (j + 1) * B, :].astype(F32)
    rate = rate_ref[...]
    rhat = rhat_ref[...]
    lane = lanes(rate.shape)
    lane_f = lane.astype(F32)
    e0 = jnp.exp(-rate * lane_f)
    e3 = jnp.exp(-rate * (B - 1.0 - lane_f))
    lam = jnp.exp(-rate)

    for copy in halo:
        copy.wait()
    ext[0, 0:8, :] = hq[0].astype(F32)[8:16] * has_prev
    for i in (1, 2):
        full = hkv[i - 1].astype(F32) * has_prev
        hext[i - 1] = full
        ext[i, 0:8, :] = full[136:144]
    qext[0, 0:8, :] = ext[0, rows : rows + 8, :]
    qext[0, 8 : 8 + B, :] = nq[0].astype(F32)
    for j in range(count):
        for i in range(3):
            feat[i, j * B : (j + 1) * B, :] = filtered(ext, i, i, 8 + j * B, B)
    head[...] = filtered(hext, 1, 0, 16, B) * filtered(hext, 2, 1, 16, B)
    tail[...] = filtered(qext, 0, 0, 8, B) * ncot[...].astype(F32) * has_next

    sub = 16

    def to_groups(t, _):
        products, grads = [], []
        for j in range(count):
            here = pl.ds(pl.multiple_of(j * B + t * sub, sub), sub)
            products.append(feat[1, here, :] * feat[2, here, :])
            grads.append(cot[here, :].astype(F32) * feat[0, here, :])
        there = pl.ds(pl.multiple_of(t * sub, sub), sub)
        for g, y in enumerate(block_transpose(products, per)):
            yp[g, there, :] = y
        for g, y in enumerate(block_transpose(grads, per)):
            yg[g, there, :] = y
        return 0

    lax.fori_loop(0, B // sub, to_groups, 0)

    for g in range(groups):
        at = slice(g * modes, (g + 1) * modes)
        s_all[at, :] = dot(e3[at], yp[g], 1, 0)
        u_all[at, :] = dot(e0[at], yg[g], 1, 0)

    state = s_all[...]
    adj = u_all[...]
    u = adj
    step = 1
    while step < count:
        decay = jnp.exp(-rate * float(B * step))
        width = per * step
        state = state + decay * jnp.where(lane >= width, rolled(state, width), 0.0)
        adj = adj + decay * jnp.where(lane < chans - width, rolled(adj, -width), 0.0)
        step *= 2
    starts = jnp.where(lane >= per, rolled(state, per), 0.0)
    ends = jnp.where(lane < chans - per, rolled(adj, -per), 0.0)

    small = lanes((modes, chans)) // per
    final = jnp.zeros((modes, chans), F32)
    first = jnp.zeros((modes, chans), F32)
    for g in range(groups):
        at = slice(g * modes, (g + 1) * modes)
        final = jnp.where(small == g, rolled(state[at], g * per - (count - 1) * per), final)
        first = jnp.where(small == g, rolled(adj[at], g * per), first)
    msg1[0:modes, :] = final
    msg1[modes : 2 * modes, :] = first
    got1[me] = msg1[...]
    sent = []
    for k in range(1, n):
        sent.append(send(msg1, got1.at[me], m1s.at[k], m1r.at[me], lax.rem(me + k, n)))

    up = jnp.exp(rate * lane_f)
    local = lam * starts * u
    terms = jnp.zeros((modes, chans), F32)
    square_l = lanes((B, B))
    square_s = lax.broadcasted_iota(jnp.int32, (B, B), 0)
    for g in range(groups):
        at = slice(g * modes, (g + 1) * modes)
        cross = dot(yg[g], yp[g], 1, 1)
        cross = jnp.where(square_s >= square_l, cross, 0.0)
        inner = dot(up[at], cross, 1, 1) * e0[at] + local[at]
        terms = jnp.where(small == g, jnp.sum(inner, axis=1, keepdims=True), terms)
    msg2[...] = terms
    got2[me] = terms
    for k in range(1, n):
        sent.append(send(msg2, got2.at[me], m2s.at[k], m2r.at[me], lax.rem(me + k, n)))

    wide = lanes((B, 2 * B))
    for g in range(groups):
        def band(which):
            row = jnp.broadcast_to(w_ref[which, g : g + 1, :], (B, 2 * B))
            return pltpu.roll(row, 0, 1, stride=1, stride_axis=0)

        fwd = band(0) + jnp.where(wide >= B, band(1), 0.0)
        bwd = band(2) + jnp.where(wide < B, band(3), 0.0)
        cur = yp[g]
        prev = jnp.where(square_l >= per, rolled(cur, per), rolled(head[...], -g * per))
        of[g] = dot(fwd[:, :B], prev, 1, 0) + dot(fwd[:, B:], cur, 1, 0)
        cur = yg[g]
        after = jnp.where(
            square_l < chans - per, rolled(cur, -per), rolled(tail[...], chans - per - g * per)
        )
        ob[g] = dot(bwd[:, :B], cur, 1, 0) + dot(bwd[:, B:], after, 1, 0)

    for k in range(1, n):
        peer = lax.rem(me + k, n)
        pltpu.make_async_remote_copy(
            src_ref=msg1, dst_ref=got1.at[peer], send_sem=m1s.at[k], recv_sem=m1r.at[peer],
            device_id={"ctx": peer}, device_id_type=MESH,
        ).wait_recv()

    whole = jnp.exp(-ratec_ref[...] * float(rows))
    lamc = jnp.exp(-ratec_ref[...])
    zero = jnp.zeros((modes, chans), F32)
    run, carry, crossed = zero, zero, zero
    for d in range(n):
        block = got1[d]
        carry = jnp.where(me == d, run, carry)
        crossed = crossed + run * block[modes:]
        run = whole * run + block[:modes]
    run, back = zero, zero
    for d in reversed(range(n)):
        back = jnp.where(me == d, run, back)
        run = whole * run + got1[d][modes:]
    crossed = crossed * lamc

    def spread(x):
        pieces = []
        for g in range(groups):
            pieces.append(jnp.where(small == 0, rolled(x, -g * per), 0.0))
        y = jnp.concatenate(pieces, axis=0)
        width = per
        while width < chans:
            y = y + rolled(y, width)
            width *= 2
        return y

    block_f = (lane // per).astype(F32)
    starts = rhat * (starts + jnp.exp(-rate * (B * block_f)) * spread(carry))
    ends = rhat * (ends + jnp.exp(-rate * (B * (count - 1.0 - block_f))) * spread(back))
    e1 = e0 * lam
    e2 = e3 * lam
    for g in range(groups):
        at = slice(g * modes, (g + 1) * modes)
        of[g] = of[g] + dot(e1[at], starts[at], 0, 0)
        ob[g] = ob[g] + dot(e2[at], ends[at], 0, 0)

    def from_groups(t, _):
        there = pl.ds(pl.multiple_of(t * sub, sub), sub)
        mixed = block_transpose([of[g, there, :] for g in range(groups)], per)
        grads = block_transpose([ob[g, there, :] for g in range(groups)], per)
        for j in range(count):
            here = pl.ds(pl.multiple_of(j * B + t * sub, sub), sub)
            mixed_out[here, :] = (feat[0, here, :] * mixed[j]).astype(BF16)
            gf[0, here, :] = cot[here, :].astype(F32) * mixed[j]
            gf[1, here, :] = grads[j] * feat[2, here, :]
            gf[2, here, :] = grads[j] * feat[1, here, :]
        return 0

    lax.fori_loop(0, B // sub, from_groups, 0)
    last = send(gf.at[:, 0:8], gfr, gs, gr, prv)

    def adjoint(i, start, size):
        total = tap[i][0] * gf[i, start : start + size, :]
        for k in range(1, short):
            total = total + tap[i][k] * gf[i, start + k : start + k + size, :]
        return total

    for j in range(count - 1):
        for i in range(3):
            grad_out[i, j * B : (j + 1) * B, :] = adjoint(i, j * B, B).astype(BF16)
    for k in range(1, n):
        peer = lax.rem(me + k, n)
        pltpu.make_async_remote_copy(
            src_ref=msg2, dst_ref=got2.at[peer], send_sem=m2s.at[k], recv_sem=m2r.at[peer],
            device_id={"ctx": peer}, device_id_type=MESH,
        ).wait_recv()
    total = got2[0]
    for d in range(1, n):
        total = total + got2[d]
    summed = zero
    for g in range(groups):
        part = jnp.sum(jnp.where(small == g, crossed, 0.0), axis=1, keepdims=True)
        summed = jnp.where(small == g, part, summed)
    res_out[...] = total + summed
    last.wait()
    gf[:, rows : rows + 8, :] = gfr[...] * has_next
    for i in range(3):
        grad_out[i, rows - B : rows, :] = adjoint(i, rows - B, B).astype(BF16)
    for copy in sent:
        copy.wait_send()


def body(n, raw_streams, short_taps, decay_rate, residue, medium_filter, cotangent):
    rows, _, chans = raw_streams.shape
    groups, modes = decay_rate.shape
    per = chans // groups
    raw = jnp.transpose(raw_streams, (1, 0, 2))
    taps = jnp.transpose(short_taps, (1, 0, 2))
    scaled = jnp.sqrt(-jnp.expm1(-2.0 * decay_rate))
    rhat = residue * scaled
    lag = jnp.arange(B, dtype=jnp.int32).astype(F32)
    h = jnp.sum(rhat[:, :, None] * jnp.exp(-decay_rate[:, :, None] * lag), axis=1)

    def reverse(v):
        return jnp.pad(v[:, ::-1], ((0, 0), (1, B - 1)))

    def plain(v):
        return jnp.pad(v, ((0, 0), (0, B)))

    w = jnp.stack([reverse(medium_filter), reverse(h), plain(medium_filter), plain(h)])
    rate_rows = jnp.broadcast_to(decay_rate.reshape(groups * modes, 1), (groups * modes, B))
    rhat_rows = jnp.broadcast_to(rhat.reshape(groups * modes, 1), (groups * modes, B))
    rate_cols = jnp.repeat(decay_rate.T, per, axis=1)
    vm = pltpu.VMEM
    dma = pltpu.SemaphoreType.DMA
    spec = pl.BlockSpec(memory_space=pltpu.VMEM)
    mixed, grads, res = pl.pallas_call(
        functools.partial(kernel, n, groups, modes),
        out_shape=(
            jax.ShapeDtypeStruct((rows, chans), BF16),
            jax.ShapeDtypeStruct((3, rows, chans), BF16),
            jax.ShapeDtypeStruct((modes, chans), F32),
        ),
        in_specs=[spec] * 7,
        out_specs=(spec, spec, spec),
        scratch_shapes=[
            vm((2, 144, chans), BF16), vm((1, 16, chans), BF16),
            vm((1, B, chans), BF16), vm((B, chans), BF16),
            vm((3, rows + 8, chans), F32), vm((3, rows, chans), F32),
            vm((2, 144, chans), F32), vm((1, B + 8, chans), F32),
            vm((groups, B, chans), F32), vm((groups, B, chans), F32),
            vm((B, chans), F32), vm((B, chans), F32),
            vm((groups * modes, chans), F32), vm((groups * modes, chans), F32),
            vm((2 * modes, chans), F32), vm((modes, chans), F32),
            vm((n, 2 * modes, chans), F32), vm((n, modes, chans), F32),
            vm((groups, B, chans), F32), vm((groups, B, chans), F32),
            vm((3, rows + 8, chans), F32), vm((3, 8, chans), F32),
            dma((4,)), dma((4,)), dma((n,)), dma((n,)), dma((n,)), dma((n,)), dma, dma,
        ],
        compiler_params=pltpu.CompilerParams(
            collective_id=0, has_side_effects=True, vmem_limit_bytes=48 * 2**20
        ),
    )(raw, taps, cotangent, rate_rows, rhat_rows, rate_cols, w)
    grad_residue = res[:, ::per].T * scaled / math.sqrt(float(rows * n * per))
    return mixed, jnp.transpose(grads, (1, 0, 2)), grad_residue


def solution(mesh):
    in_specs = (
        P(("dp", "ctx"), None, "ch"),
        P(None, None, "ch"),
        P("ch", None),
        P("ch", None),
        P("ch", None),
        P(("dp", "ctx"), "ch"),
    )
    out_specs = (P(("dp", "ctx"), "ch"), P(("dp", "ctx"), None, "ch"), P(("dp", "ch"), None))
    return jax.shard_map(
        functools.partial(body, mesh.shape["ctx"]),
        mesh=mesh, in_specs=in_specs, out_specs=out_specs, check_vma=False,
    )
```

time: 288 us -> 33.7 us (0.12); the launches traced: 285 us -> 33.4 us
  local copies, waits for them, and re-layouts: 97.7 us -> 6.3 us
  matrix products: 85.4 us -> 0 us
  blocking collectives: 53.8 us -> 0 us
  other arithmetic: 34.6 us -> 0.16 us
  Pallas kernels: 0 us -> 26.2 us
  starting transfers between devices: 11.1 us -> 0 us
    dot_general x83 -> x0, matrix products: 85.4 us -> none  [einsum_high(): return jnp.einsum(form, *operands, precision=lax.Precision.HIGHEST)]
    dynamic_update_slice x24 -> x0, local copies, waits for them, and re-layouts: 49.9 us -> none  [forward_blocks(): _, (outputs, starts) = lax.scan(forward_step, state_init, (pieces, prevs))]
    all_gather x1 -> x0, blocking collectives: 32.9 us -> none  [body(): piece = lax.all_gather(paired, 'ctx', axis=0, tiled=True)]
    dynamic_slice x24 -> x0, local copies, waits for them, and re-layouts: 26.5 us -> none  [forward_blocks(): _, (outputs, starts) = lax.scan(forward_step, state_init, (pieces, prevs))]
    pallas_call x0 -> x1, Pallas kernels: none -> 26.2 us  [body(): pl.pallas_call(functools.partial(kernel, n, groups, modes), out_shape=(ja...]
    psum x1 -> x0, blocking collectives: 20.9 us -> none  [body(): summed = lax.psum(running, 'ctx')]
    dot_general x9 -> x0, other arithmetic: 18.1 us -> none  [einsum_high(): return jnp.einsum(form, *operands, precision=lax.Precision.HIGHEST)]
    ppermute x4 -> x0, starting transfers between devices: 11.1 us -> none  [shifted(): return lax.ppermute(block, axis, route)]
  transfers between devices with their start and end apart: 4 -> 0, of which waited for: 0 -> 0; matrix products, arithmetic and copies ran while one was open for 35% -> 0% of each run, Pallas kernels for 0% -> 0%
where the time goes in v1:
time: 33.7 us; the launch traced here: 33.4 us
  Pallas kernels  26.2 us (78%)
  local copies, waits for them, and re-layouts  6.3 us (19%)
  between operations  0.69 us (2%)
    pallas_call x1, Pallas kernels, body(): pl.pallas_call(functools.partial(kernel, n, groups, modes), out_shape=(ja...  26.2 us
    unnamed x17, local copies, waits for them, and re-layouts  5.38 us

profile of v1, /device:TPU:0, one launch (start us, length us, event | category | flops | bytes accessed | tf_op | source)
XLA Modules:
  0.0 33.4 jit_solution(15492194139781222316)
XLA Ops:
  0.6 0.8 %copy.21 = f32[8,16]{0,1:T(8,128)S(1)} copy(f32[8,16]{1,0:T(8,128)} %param.8) | data formatting | bytes 1024 | tf_op args[2]
  1.4 0.0 copy-done.5
  1.4 0.1 copy.23
  1.5 0.1 copy.24
  1.6 0.5 %copy-done.3 = f32[8,16]{1,0:T(8,128)S(1)} copy-done((f32[8,16]{1,0:T(8,128)S(1)}, f32[8,16]{1,0:T(8,128)}, u32[]{:S(2)}) %copy-start.3) | copy-done | bytes 536
  2.1 0.1 multiply_reduce_fusion
  2.2 0.1 rev.7
  2.3 0.1 rev.6
  2.4 0.1 pad_bitcast_fusion.2
  2.4 0.1 broadcast_in_dim.22
  2.5 0.1 broadcast_in_dim.23.rhat_ref
  2.6 0.1 copy.25
  2.7 0.1 broadcast_in_dim.24
  2.8 0.1 reshape.20.ratec_ref
  2.9 0.1 broadcast_in_dim.20
  2.9 0.1 broadcast_in_dim.21.rate_ref
  3.0 0.0 copy-done.1
  3.0 0.6 %copy-done.2 = f32[7,3,128]{2,0,1:T(8,128)S(1)} copy-done((f32[7,3,128]{2,0,1:T(8,128)S(1)}, f32[7,3,128]{2,0,1:T(8,128)}, u32[]{:S(2)}) %copy-start.2) | copy-done | bytes 10776
  3.7 1.1 %copy-done = bf16[1024,3,128]{2,0,1:T(8,128)(2,1)S(1)} copy-done((bf16[1024,3,128]{2,0,1:T(8,128)(2,1)S(1)}, bf16[1024,3,128]{2,0,1:T(8,128)(2,1)}, u32[]{:S(2)}) %copy-start) | copy-done | bytes 786456
  4.8 26.2 %shard_map.85 = (bf16[1024,128]{1,0:T(8,128)(2,1)S(1)}, bf16[3,1024,128]{2,1,0:T(8,128)(2,1)S(1)}, f32[16,128]{1,0:T(8,128)S(1)}) custom-call(bf16[3,1024,128]{2,1,0:T(8,128)(2,1)S(1)} %bitcast.16, f32[3,7,128]{2,1,0:T(8,128)S(1)} %bitcast.18, bf16[1024,128]{1,0:T(8,128)(2,1)S(1)} %copy-done.1, f32[128,128]{1,0:T(8,128)S(1)} %broadcast_in_dim.21.rate_ref, ...), custom_call_target="tpu_custom_call" | custom-call | tf_op jit(solution)/shard_map/pallas_call | solution.py:317
  31.0 0.1 slice.3
  31.1 0.7 %copy.27 = f32[8,16]{1,0:T(8,128)} copy(f32[8,16]{0,1:T(8,128)S(1)} %fusion) | data formatting | bytes 1024
  31.8 0.7 %copy.30 = bf16[1024,128]{1,0:T(8,128)(2,1)} copy(bf16[1024,128]{1,0:T(8,128)(2,1)S(1)} %get-tuple-element.25) | data formatting | bytes 524288
  32.5 0.9 %copy.31 = bf16[1024,3,128]{2,0,1:T(8,128)(2,1)} copy(bf16[1024,3,128]{2,0,1:T(8,128)(2,1)S(1)} %bitcast.17) | data formatting | bytes 1572864
  (13 shorter events, 0.1 us)
Async XLA Ops:
  0.6 0.8 %copy-start.5 = (f32[8,16]{1,0:T(8,128)S(1)}, f32[8,16]{1,0:T(8,128)}, u32[]{:S(2)}) copy-start(f32[8,16]{1,0:T(8,128)} %param.9) | copy-start | bytes 1540
  1.4 0.7 %copy-start.3 = (f32[8,16]{1,0:T(8,128)S(1)}, f32[8,16]{1,0:T(8,128)}, u32[]{:S(2)}) copy-start(f32[8,16]{1,0:T(8,128)} %param.8) | copy-start | bytes 1540
  1.4 0.9 %copy-start.4 = (f32[8,128]{1,0:T(8,128)S(1)}, f32[8,128]{1,0:T(8,128)}, u32[]{:S(2)}) copy-start(f32[8,128]{1,0:T(8,128)} %param.10) | copy-start | bytes 12292
  1.5 1.5 %copy-start.1 = (bf16[1024,128]{1,0:T(8,128)(2,1)S(1)}, bf16[1024,128]{1,0:T(8,128)(2,1)}, u32[]{:S(2)}) copy-start(bf16[1024,128]{1,0:T(8,128)(2,1)} %cot.1) | copy-start | bytes 786436
  2.9 0.7 %copy-start.2 = (f32[7,3,128]{2,0,1:T(8,128)S(1)}, f32[7,3,128]{2,0,1:T(8,128)}, u32[]{:S(2)}) copy-start(f32[7,3,128]{2,0,1:T(8,128)} %param.7) | copy-start | bytes 32260
  3.7 1.1 %copy-start = (bf16[1024,3,128]{2,0,1:T(8,128)(2,1)S(1)}, bf16[1024,3,128]{2,0,1:T(8,128)(2,1)}, u32[]{:S(2)}) copy-start(bf16[1024,3,128]{2,0,1:T(8,128)(2,1)} %param.6) | copy-start | bytes 2359300

commit v2 on v1

--- a/solution.py
+++ b/solution.py
@@ -12,13 +12,25 @@
 BF16 = jnp.bfloat16
 MESH = pl.DeviceIdType.MESH
 B = 128
-HIGH = lax.Precision.HIGHEST
-
-
-def dot(a, b, ca, cb):
-    return lax.dot_general(
-        a, b, (((ca,), (cb,)), ((), ())), precision=HIGH, preferred_element_type=F32
-    )
+
+
+def halves(x):
+    hi = x.astype(BF16)
+    return hi, (x - hi.astype(F32)).astype(BF16)
+
+
+def quadrants(a, b, cb):
+    out = lax.dot_general(a, b, (((1,), (cb,)), ((), ())), preferred_element_type=F32)
+    r, c = out.shape[0] // 2, out.shape[1] // 2
+    return (out[:r, :c] + out[:r, c:]) + (out[r:, :c] + out[r:, c:])
+
+
+def tall(x):
+    return jnp.concatenate(halves(x), axis=0)
+
+
+def flat(x):
+    return jnp.concatenate(halves(x), axis=1)
 
 
 def lanes(shape):
@@ -48,8 +60,9 @@
 
 def kernel(
     n, groups, modes,
-    raw, taps, cot, rate_ref, rhat_ref, ratec_ref, w_ref,
+    raw_hbm, taps, cot_hbm, rate_ref, rhat_ref, rev_ref, med_ref,
     mixed_out, grad_out, res_out,
+    raw, cot, tf, tb, ls,
     hkv, hq, nq, ncot, ext, feat, hext, qext, yp, yg, head, tail,
     s_all, u_all, msg1, msg2, got1, got2, of, ob, gf, gfr,
     hs, hr, m1s, m1r, m2s, m2r, gs, gr,
@@ -58,6 +71,10 @@
     per = chans // groups
     count = rows // B
     short = taps.shape[1]
+    loads = [pltpu.make_async_copy(raw_hbm.at[i], raw.at[i], ls.at[i]) for i in range(3)]
+    loads.append(pltpu.make_async_copy(cot_hbm, cot, ls.at[3]))
+    for i in (1, 2, 0, 3):
+        loads[i].start()
     me = lax.axis_index("ctx")
     nxt = lax.rem(me + 1, n)
     prv = lax.rem(me + n - 1, n)
@@ -77,10 +94,10 @@
         return copy
 
     halo = [
-        send(raw.at[0:1, rows - 16 : rows], hq, hs.at[0], hr.at[0], nxt),
-        send(raw.at[1:3, rows - 144 : rows], hkv, hs.at[1], hr.at[1], nxt),
-        send(raw.at[0:1, 0:B], nq, hs.at[2], hr.at[2], prv),
-        send(cot.at[0:B], ncot, hs.at[3], hr.at[3], prv),
+        send(raw_hbm.at[0:1, rows - 16 : rows], hq, hs.at[0], hr.at[0], nxt),
+        send(raw_hbm.at[1:3, rows - 144 : rows], hkv, hs.at[1], hr.at[1], nxt),
+        send(raw_hbm.at[0:1, 0:B], nq, hs.at[2], hr.at[2], prv),
+        send(cot_hbm.at[0:B], ncot, hs.at[3], hr.at[3], prv),
     ]
 
     has_prev = jnp.where(me > 0, 1.0, 0.0).astype(F32)
@@ -93,16 +110,56 @@
             total = total + tap[i][k] * ref[slot, start - k : start - k + size, :]
         return total
 
-    for j in range(count):
-        for i in range(3):
-            ext[i, 8 + j * B : 8 + (j + 1) * B, :] = raw[i, j * B : (j + 1) * B, :].astype(F32)
-    rate = rate_ref[...]
-    rhat = rhat_ref[...]
+    def expanded(ref):
+        tile = jnp.concatenate(
+            [jnp.broadcast_to(ref[g : g + 1, :], (modes, modes)) for g in range(groups)], axis=0
+        )
+        row = lax.broadcasted_iota(jnp.int32, tile.shape, 0) % modes
+        column = jnp.sum(jnp.where(lanes(tile.shape) == row, tile, 0.0), axis=1, keepdims=True)
+        return jnp.broadcast_to(column, (groups * modes, B))
+
+    rate = expanded(rate_ref)
+    rhat = expanded(rhat_ref)
     lane = lanes(rate.shape)
     lane_f = lane.astype(F32)
     e0 = jnp.exp(-rate * lane_f)
+    e2 = jnp.exp(-rate * (B - lane_f))
     e3 = jnp.exp(-rate * (B - 1.0 - lane_f))
     lam = jnp.exp(-rate)
+    sub_i = lax.broadcasted_iota(jnp.int32, rate.shape, 0)
+    sub_f = sub_i.astype(F32)
+    rate_row = jnp.sum(jnp.where(sub_i == lane, rate, 0.0), axis=0, keepdims=True)
+    e1t = flat(jnp.exp(-rate_row * (sub_f + 1.0)))
+    e2t = flat(jnp.exp(-rate_row * (B - sub_f)))
+    square_l, square_s = lane, sub_i
+
+    wide = lanes((B, 2 * B))
+    for g in range(groups):
+        at = slice(g * modes, (g + 1) * modes)
+        hb = jnp.sum(rhat[at] * e0[at], axis=0, keepdims=True)
+        hf = jnp.sum(rhat[at] * e2[at], axis=0, keepdims=True)
+        row_l = lanes(hb.shape)
+        zrow = jnp.zeros_like(hb)
+        hf = jnp.where(row_l == 0, 0.0, hf)
+        first_h = jnp.where(row_l == 0, hb, 0.0)
+
+        def band(row):
+            row = jnp.broadcast_to(row, (B, 2 * B))
+            return pltpu.roll(row, 0, 1, stride=1, stride_axis=0)
+
+        fwd_h = band(jnp.concatenate([hf, first_h], axis=1))
+        bwd_h = band(jnp.concatenate([hb, zrow], axis=1))
+        bwd_m = band(jnp.concatenate([med_ref[g : g + 1, :], zrow], axis=1))
+        tf[g] = tall(band(rev_ref[g : g + 1, :]) + jnp.where(wide >= B, fwd_h, 0.0))
+        tb[g] = tall(bwd_m + jnp.where(wide < B, bwd_h, 0.0))
+
+    for i in (1, 2, 0):
+        loads[i].wait()
+        for j in range(count):
+            ext[i, 8 + j * B : 8 + (j + 1) * B, :] = raw[i, j * B : (j + 1) * B, :].astype(F32)
+        for j in range(1, count):
+            feat[i, j * B : (j + 1) * B, :] = filtered(ext, i, i, 8 + j * B, B)
+    loads[3].wait()
 
     for copy in halo:
         copy.wait()
@@ -113,9 +170,8 @@
         ext[i, 0:8, :] = full[136:144]
     qext[0, 0:8, :] = ext[0, rows : rows + 8, :]
     qext[0, 8 : 8 + B, :] = nq[0].astype(F32)
-    for j in range(count):
-        for i in range(3):
-            feat[i, j * B : (j + 1) * B, :] = filtered(ext, i, i, 8 + j * B, B)
+    for i in range(3):
+        feat[i, 0:B, :] = filtered(ext, i, i, 8, B)
     head[...] = filtered(hext, 1, 0, 16, B) * filtered(hext, 2, 1, 16, B)
     tail[...] = filtered(qext, 0, 0, 8, B) * ncot[...].astype(F32) * has_next
 
@@ -134,12 +190,12 @@
             yg[g, there, :] = y
         return 0
 
-    lax.fori_loop(0, B // sub, to_groups, 0)
+    lax.fori_loop(0, B // sub, to_groups, 0, unroll=B // sub)
 
     for g in range(groups):
         at = slice(g * modes, (g + 1) * modes)
-        s_all[at, :] = dot(e3[at], yp[g], 1, 0)
-        u_all[at, :] = dot(e0[at], yg[g], 1, 0)
+        s_all[at, :] = quadrants(tall(e3[at]), flat(yp[g]), 0)
+        u_all[at, :] = quadrants(tall(e0[at]), flat(yg[g]), 0)
 
     state = s_all[...]
     adj = u_all[...]
@@ -171,35 +227,26 @@
     up = jnp.exp(rate * lane_f)
     local = lam * starts * u
     terms = jnp.zeros((modes, chans), F32)
-    square_l = lanes((B, B))
-    square_s = lax.broadcasted_iota(jnp.int32, (B, B), 0)
     for g in range(groups):
         at = slice(g * modes, (g + 1) * modes)
-        cross = dot(yg[g], yp[g], 1, 1)
+        cross = quadrants(tall(yg[g]), tall(yp[g]), 1)
         cross = jnp.where(square_s >= square_l, cross, 0.0)
-        inner = dot(up[at], cross, 1, 1) * e0[at] + local[at]
+        inner = quadrants(tall(up[at]), tall(cross), 1) * e0[at] + local[at]
         terms = jnp.where(small == g, jnp.sum(inner, axis=1, keepdims=True), terms)
     msg2[...] = terms
     got2[me] = terms
     for k in range(1, n):
         sent.append(send(msg2, got2.at[me], m2s.at[k], m2r.at[me], lax.rem(me + k, n)))
 
-    wide = lanes((B, 2 * B))
-    for g in range(groups):
-        def band(which):
-            row = jnp.broadcast_to(w_ref[which, g : g + 1, :], (B, 2 * B))
-            return pltpu.roll(row, 0, 1, stride=1, stride_axis=0)
-
-        fwd = band(0) + jnp.where(wide >= B, band(1), 0.0)
-        bwd = band(2) + jnp.where(wide < B, band(3), 0.0)
+    for g in range(groups):
         cur = yp[g]
         prev = jnp.where(square_l >= per, rolled(cur, per), rolled(head[...], -g * per))
-        of[g] = dot(fwd[:, :B], prev, 1, 0) + dot(fwd[:, B:], cur, 1, 0)
+        of[g] = quadrants(tf[g], jnp.concatenate([flat(prev), flat(cur)], axis=0), 0)
         cur = yg[g]
         after = jnp.where(
             square_l < chans - per, rolled(cur, -per), rolled(tail[...], chans - per - g * per)
         )
-        ob[g] = dot(bwd[:, :B], cur, 1, 0) + dot(bwd[:, B:], after, 1, 0)
+        ob[g] = quadrants(tb[g], jnp.concatenate([flat(cur), flat(after)], axis=0), 0)
 
     for k in range(1, n):
         peer = lax.rem(me + k, n)
@@ -208,8 +255,11 @@
             device_id={"ctx": peer}, device_id_type=MESH,
         ).wait_recv()
 
-    whole = jnp.exp(-ratec_ref[...] * float(rows))
-    lamc = jnp.exp(-ratec_ref[...])
+    rate_c = jnp.zeros((modes, chans), F32)
+    for g in range(groups):
+        rate_c = jnp.where(small == g, rate[g * modes : (g + 1) * modes], rate_c)
+    whole = jnp.exp(-rate_c * float(rows))
+    lamc = jnp.exp(-rate_c)
     zero = jnp.zeros((modes, chans), F32)
     run, carry, crossed = zero, zero, zero
     for d in range(n):
@@ -237,12 +287,25 @@
     block_f = (lane // per).astype(F32)
     starts = rhat * (starts + jnp.exp(-rate * (B * block_f)) * spread(carry))
     ends = rhat * (ends + jnp.exp(-rate * (B * (count - 1.0 - block_f))) * spread(back))
-    e1 = e0 * lam
-    e2 = e3 * lam
-    for g in range(groups):
-        at = slice(g * modes, (g + 1) * modes)
-        of[g] = of[g] + dot(e1[at], starts[at], 0, 0)
-        ob[g] = ob[g] + dot(e2[at], ends[at], 0, 0)
+    starts = flat(starts)
+    ends = flat(ends)
+
+    def carried(table, state, g):
+        parts = [state[g * modes : (g + 1) * modes]]
+        if g:
+            parts.insert(0, jnp.zeros((g * modes, 2 * chans), BF16))
+        if g < groups - 1:
+            parts.append(jnp.zeros(((groups - 1 - g) * modes, 2 * chans), BF16))
+        z = jnp.concatenate(parts, axis=0)
+        out = lax.dot_general(
+            table, jnp.concatenate([z, z], axis=0), (((1,), (0,)), ((), ())),
+            preferred_element_type=F32,
+        )
+        return out[:, :chans] + out[:, chans:]
+
+    for g in range(groups):
+        of[g] = of[g] + carried(e1t, starts, g)
+        ob[g] = ob[g] + carried(e2t, ends, g)
 
     def from_groups(t, _):
         there = pl.ds(pl.multiple_of(t * sub, sub), sub)
@@ -256,7 +319,7 @@
             gf[2, here, :] = grads[j] * feat[1, here, :]
         return 0
 
-    lax.fori_loop(0, B // sub, from_groups, 0)
+    lax.fori_loop(0, B // sub, from_groups, 0, unroll=B // sub)
     last = send(gf.at[:, 0:8], gfr, gs, gr, prv)
 
     def adjoint(i, start, size):
@@ -298,21 +361,10 @@
     taps = jnp.transpose(short_taps, (1, 0, 2))
     scaled = jnp.sqrt(-jnp.expm1(-2.0 * decay_rate))
     rhat = residue * scaled
-    lag = jnp.arange(B, dtype=jnp.int32).astype(F32)
-    h = jnp.sum(rhat[:, :, None] * jnp.exp(-decay_rate[:, :, None] * lag), axis=1)
-
-    def reverse(v):
-        return jnp.pad(v[:, ::-1], ((0, 0), (1, B - 1)))
-
-    def plain(v):
-        return jnp.pad(v, ((0, 0), (0, B)))
-
-    w = jnp.stack([reverse(medium_filter), reverse(h), plain(medium_filter), plain(h)])
-    rate_rows = jnp.broadcast_to(decay_rate.reshape(groups * modes, 1), (groups * modes, B))
-    rhat_rows = jnp.broadcast_to(rhat.reshape(groups * modes, 1), (groups * modes, B))
-    rate_cols = jnp.repeat(decay_rate.T, per, axis=1)
+    rev = jnp.pad(medium_filter[:, ::-1], ((0, 0), (1, B - 1)))
     vm = pltpu.VMEM
     dma = pltpu.SemaphoreType.DMA
+    hbm = pl.BlockSpec(memory_space=pltpu.HBM)
     spec = pl.BlockSpec(memory_space=pltpu.VMEM)
     mixed, grads, res = pl.pallas_call(
         functools.partial(kernel, n, groups, modes),
@@ -321,9 +373,11 @@
             jax.ShapeDtypeStruct((3, rows, chans), BF16),
             jax.ShapeDtypeStruct((modes, chans), F32),
         ),
-        in_specs=[spec] * 7,
+        in_specs=[hbm, spec, hbm, spec, spec, spec, spec],
         out_specs=(spec, spec, spec),
         scratch_shapes=[
+            vm((3, rows, chans), BF16), vm((rows, chans), BF16),
+            vm((groups, 2 * B, 2 * B), BF16), vm((groups, 2 * B, 2 * B), BF16), dma((4,)),
             vm((2, 144, chans), BF16), vm((1, 16, chans), BF16),
             vm((1, B, chans), BF16), vm((B, chans), BF16),
             vm((3, rows + 8, chans), F32), vm((3, rows, chans), F32),
@@ -340,7 +394,7 @@
         compiler_params=pltpu.CompilerParams(
             collective_id=0, has_side_effects=True, vmem_limit_bytes=48 * 2**20
         ),
-    )(raw, taps, cotangent, rate_rows, rhat_rows, rate_cols, w)
+    )(raw, taps, cotangent, decay_rate, rhat, rev, medium_filter)
     grad_residue = res[:, ::per].T * scaled / math.sqrt(float(rows * n * per))
     return mixed, jnp.transpose(grads, (1, 0, 2)), grad_residue
 

time: 33.7 us -> 28.8 us (0.85)
  Pallas kernels: 26.2 us -> 21.9 us
  local copies, waits for them, and re-layouts: 6.3 us -> 4.55 us
  other arithmetic: 0.16 us -> 1.34 us
    pallas_call x1, Pallas kernels: 26.2 us -> 21.9 us  [body(): pl.pallas_call(functools.partial(kernel, n, groups, modes), out_shape=(ja...]
    unnamed x17 -> x12, local copies, waits for them, and re-layouts: 5.38 us -> 4.28 us
    mul x1, other arithmetic: 0.02 us -> 0.72 us  [body(): rhat = residue * scaled]
    div x1, other arithmetic: 0.03 us -> 0.62 us  [body(): grad_residue = res[:, ::per].T * scaled / math.sqrt(float(rows * n * per))]
    broadcast_in_dim x5 -> x0, local copies, waits for them, and re-layouts: 0.38 us -> none  [the longest x2 0.15 us: body(): jnp.broadcast_to(rhat.reshape(groups * modes, 1), (groups * modes, B))]
where the time goes in v2:
time: 28.8 us; the launch traced here: 28.5 us
  Pallas kernels  21.9 us (76%)
  local copies, waits for them, and re-layouts  4.55 us (16%)
  other arithmetic  1.34 us (5%)
  between operations  0.67 us (2%)
    pallas_call x1, Pallas kernels, body(): pl.pallas_call(functools.partial(kernel, n, groups, modes), out_shape=(ja...  21.9 us
    unnamed x12, local copies, waits for them, and re-layouts  4.28 us
    mul x1, other arithmetic, body(): rhat = residue * scaled  0.72 us
    div x1, other arithmetic, body(): grad_residue = res[:, ::per].T * scaled / math.sqrt(float(rows * n * per))  0.62 us

profile of v2, /device:TPU:0, one launch (start us, length us, event | category | flops | bytes accessed | tf_op | source)
XLA Modules:
  0.0 28.5 jit_solution(17680133770100668087)
XLA Ops:
  0.6 0.0 copy-start.3
  0.6 0.7 %fusion.1.rhat_ref = f32[8,16]{1,0:T(8,128)S(1)} fusion(f32[8,16]{1,0:T(8,128)} %param.9, f32[8,16]{1,0:T(8,128)} %rate_ref.1), kind=kLoop, calls=%fused_computation.3 | loop fusion | flops 384 | bytes 1536 | tf_op jit(solution)/shard_map/mul | solution.py:363
  1.4 0.0 copy-done.3
  1.4 0.0 copy-start.4
  1.4 0.1 rev.3
  1.5 0.0 copy-start.2
  1.5 0.1 pad.4.rev_ref
  1.5 0.6 %copy-done.4 = f32[7,3,128]{2,0,1:T(8,128)S(1)} copy-done((f32[7,3,128]{2,0,1:T(8,128)S(1)}, f32[7,3,128]{2,0,1:T(8,128)}, u32[]{:S(2)}) %copy-start.4) | copy-done | bytes 10776
  2.1 0.1 copy-done.2
  2.1 0.0 copy-start
  2.1 1.1 %copy-done = bf16[1024,3,128]{2,0,1:T(8,128)(2,1)S(1)} copy-done((bf16[1024,3,128]{2,0,1:T(8,128)(2,1)S(1)}, bf16[1024,3,128]{2,0,1:T(8,128)(2,1)}, u32[]{:S(2)}) %copy-start) | copy-done | bytes 786456
  3.3 0.0 copy-start.1
  3.3 0.9 %copy-done.1 = bf16[1024,128]{1,0:T(8,128)(2,1)S(1)} copy-done((bf16[1024,128]{1,0:T(8,128)(2,1)S(1)}, bf16[1024,128]{1,0:T(8,128)(2,1)}, u32[]{:S(2)}) %copy-start.1) | copy-done | bytes 262168
  4.2 21.9 %shard_map.85 = (bf16[1024,128]{1,0:T(8,128)(2,1)S(1)}, bf16[3,1024,128]{2,1,0:T(8,128)(2,1)S(1)}, f32[16,128]{1,0:T(8,128)S(1)}) custom-call(bf16[3,1024,128]{2,1,0:T(8,128)(2,1)S(1)} %bitcast.8, f32[3,7,128]{2,1,0:T(8,128)S(1)} %bitcast.9, bf16[1024,128]{1,0:T(8,128)(2,1)S(1)} %copy-done.1, f32[8,16]{1,0:T(8,128)S(1)} %copy-done.2, ...), custom_call_target="tpu_custom_call" | custom-call | tf_op jit(solution)/shard_map/pallas_call | solution.py:369
  26.2 0.1 copy.9
  26.3 0.6 %fusion = f32[8,16]{1,0:T(8,128)} fusion(f32[16,8]{0,1:T(8,128)S(1)} %slice.3, f32[8,16]{1,0:T(8,128)S(1)} %copy-done.2), kind=kLoop, calls=%fused_computation.1 | loop fusion | flops 512 | bytes 1536 | tf_op jit(solution)/shard_map/div | solution.py:398
  26.9 0.7 %copy.12 = bf16[1024,128]{1,0:T(8,128)(2,1)} copy(bf16[1024,128]{1,0:T(8,128)(2,1)S(1)} %get-tuple-element.12) | data formatting | bytes 524288
  27.6 0.9 %copy.13 = bf16[1024,3,128]{2,0,1:T(8,128)(2,1)} copy(bf16[1024,3,128]{2,0,1:T(8,128)(2,1)S(1)} %bitcast.7) | data formatting | bytes 1572864
  (1 shorter events, 0.0 us)
Async XLA Ops:
  0.6 0.7 %copy-start.3 = (f32[8,128]{1,0:T(8,128)S(1)}, f32[8,128]{1,0:T(8,128)}, u32[]{:S(2)}) copy-start(f32[8,128]{1,0:T(8,128)} %med_ref.1) | copy-start | bytes 12292
  1.4 0.7 %copy-start.4 = (f32[7,3,128]{2,0,1:T(8,128)S(1)}, f32[7,3,128]{2,0,1:T(8,128)}, u32[]{:S(2)}) copy-start(f32[7,3,128]{2,0,1:T(8,128)} %param.7) | copy-start | bytes 32260
  1.5 0.7 %copy-start.2 = (f32[8,16]{1,0:T(8,128)S(1)}, f32[8,16]{1,0:T(8,128)}, u32[]{:S(2)}) copy-start(f32[8,16]{1,0:T(8,128)} %rate_ref.1) | copy-start | bytes 1540
  2.1 1.1 %copy-start = (bf16[1024,3,128]{2,0,1:T(8,128)(2,1)S(1)}, bf16[1024,3,128]{2,0,1:T(8,128)(2,1)}, u32[]{:S(2)}) copy-start(bf16[1024,3,128]{2,0,1:T(8,128)(2,1)} %param.6) | copy-start | bytes 2359300
  3.3 0.9 %copy-start.1 = (bf16[1024,128]{1,0:T(8,128)(2,1)S(1)}, bf16[1024,128]{1,0:T(8,128)(2,1)}, u32[]{:S(2)}) copy-start(bf16[1024,128]{1,0:T(8,128)(2,1)} %cot_hbm.1) | copy-start | bytes 786436

commit v3 on v2

--- a/solution.py
+++ b/solution.py
@@ -12,6 +12,7 @@
 BF16 = jnp.bfloat16
 MESH = pl.DeviceIdType.MESH
 B = 128
+VMEM_LIMIT = 63 * 2**20
 
 
 def halves(x):
@@ -60,9 +61,9 @@
 
 def kernel(
     n, groups, modes,
-    raw_hbm, taps, cot_hbm, rate_ref, rhat_ref, rev_ref, med_ref,
-    mixed_out, grad_out, res_out,
-    raw, cot, tf, tb, ls,
+    raw_hbm, taps_hbm, cot_hbm, rate_hbm, res_hbm, med_hbm,
+    mixed_hbm, grad_hbm, out_hbm,
+    mixed_out, grad_out, res_out, ws, taps, rate_ref, residue_ref, med_ref, raw, cot, tf, tb, ls,
     hkv, hq, nq, ncot, ext, feat, hext, qext, yp, yg, head, tail,
     s_all, u_all, msg1, msg2, got1, got2, of, ob, gf, gfr,
     hs, hr, m1s, m1r, m2s, m2r, gs, gr,
@@ -73,7 +74,10 @@
     short = taps.shape[1]
     loads = [pltpu.make_async_copy(raw_hbm.at[i], raw.at[i], ls.at[i]) for i in range(3)]
     loads.append(pltpu.make_async_copy(cot_hbm, cot, ls.at[3]))
-    for i in (1, 2, 0, 3):
+    small_in = ((rate_hbm, rate_ref), (res_hbm, residue_ref), (med_hbm, med_ref), (taps_hbm, taps))
+    for i, (src, dst) in enumerate(small_in):
+        loads.append(pltpu.make_async_copy(src, dst, ls.at[4 + i]))
+    for i in (4, 5, 6, 7, 1, 2, 0, 3):
         loads[i].start()
     me = lax.axis_index("ctx")
     nxt = lax.rem(me + 1, n)
@@ -102,6 +106,8 @@
 
     has_prev = jnp.where(me > 0, 1.0, 0.0).astype(F32)
     has_next = jnp.where(me < n - 1, 1.0, 0.0).astype(F32)
+    for i in range(4, 8):
+        loads[i].wait()
     tap = [[taps[i, k : k + 1, :] for k in range(short)] for i in range(3)]
 
     def filtered(ref, i, slot, start, size):
@@ -119,7 +125,12 @@
         return jnp.broadcast_to(column, (groups * modes, B))
 
     rate = expanded(rate_ref)
-    rhat = expanded(rhat_ref)
+    twice = 2.0 * rate
+    series = 1.0 - twice / 6.0 * (1.0 - twice / 7.0)
+    for k in (5.0, 4.0, 3.0, 2.0):
+        series = 1.0 - twice / k * series
+    scaled = jnp.sqrt(jnp.where(twice < 0.2, twice * series, 1.0 - jnp.exp(-twice)))
+    rhat = expanded(residue_ref) * scaled
     lane = lanes(rate.shape)
     lane_f = lane.astype(F32)
     e0 = jnp.exp(-rate * lane_f)
@@ -133,25 +144,28 @@
     e2t = flat(jnp.exp(-rate_row * (B - sub_f)))
     square_l, square_s = lane, sub_i
 
-    wide = lanes((B, 2 * B))
+    flip = jnp.where((lane + sub_i) % B == 0, 1.0, 0.0)
+    med = med_ref[...]
+    med_rev = lax.dot_general(
+        med, flip, (((1,), (0,)), ((), ())),
+        precision=lax.Precision.HIGHEST, preferred_element_type=F32,
+    )
+    e_rev = jnp.where(lane == 0, 1.0, e2)
+
+    def band(row):
+        return pltpu.roll(jnp.broadcast_to(row, (B, B)), 0, 1, stride=1, stride_axis=0)
+
     for g in range(groups):
         at = slice(g * modes, (g + 1) * modes)
         hb = jnp.sum(rhat[at] * e0[at], axis=0, keepdims=True)
-        hf = jnp.sum(rhat[at] * e2[at], axis=0, keepdims=True)
-        row_l = lanes(hb.shape)
-        zrow = jnp.zeros_like(hb)
-        hf = jnp.where(row_l == 0, 0.0, hf)
-        first_h = jnp.where(row_l == 0, hb, 0.0)
-
-        def band(row):
-            row = jnp.broadcast_to(row, (B, 2 * B))
-            return pltpu.roll(row, 0, 1, stride=1, stride_axis=0)
-
-        fwd_h = band(jnp.concatenate([hf, first_h], axis=1))
-        bwd_h = band(jnp.concatenate([hb, zrow], axis=1))
-        bwd_m = band(jnp.concatenate([med_ref[g : g + 1, :], zrow], axis=1))
-        tf[g] = tall(band(rev_ref[g : g + 1, :]) + jnp.where(wide >= B, fwd_h, 0.0))
-        tb[g] = tall(bwd_m + jnp.where(wide < B, bwd_h, 0.0))
+        hf = jnp.sum(rhat[at] * e_rev[at], axis=0, keepdims=True)
+        mb, mf = med[g : g + 1], med_rev[g : g + 1]
+        prev = jnp.where(lane > sub_i, band(mf), 0.0)
+        cur = jnp.where(lane <= sub_i, band(mf + hf), 0.0)
+        tf[g] = tall(jnp.concatenate([prev, cur], axis=1))
+        cur = jnp.where(lane >= sub_i, band(mb + hb), 0.0)
+        after = jnp.where(lane < sub_i, band(mb), 0.0)
+        tb[g] = tall(jnp.concatenate([cur, after], axis=1))
 
     for i in (1, 2, 0):
         loads[i].wait()
@@ -320,7 +334,16 @@
         return 0
 
     lax.fori_loop(0, B // sub, from_groups, 0, unroll=B // sub)
+    writes = []
+
+    def write(src, dst):
+        copy = pltpu.make_async_copy(src, dst, ws.at[len(writes)])
+        copy.start()
+        writes.append(copy)
+
     last = send(gf.at[:, 0:8], gfr, gs, gr, prv)
+
+    write(mixed_out, mixed_hbm)
 
     def adjoint(i, start, size):
         total = tap[i][0] * gf[i, start : start + size, :]
@@ -328,9 +351,10 @@
             total = total + tap[i][k] * gf[i, start + k : start + k + size, :]
         return total
 
-    for j in range(count - 1):
-        for i in range(3):
+    for i in range(3):
+        for j in range(count - 1):
             grad_out[i, j * B : (j + 1) * B, :] = adjoint(i, j * B, B).astype(BF16)
+    write(grad_out.at[:, 0 : rows - B], grad_hbm.at[:, 0 : rows - B])
     for k in range(1, n):
         peer = lax.rem(me + k, n)
         pltpu.make_async_remote_copy(
@@ -344,13 +368,35 @@
     for g in range(groups):
         part = jnp.sum(jnp.where(small == g, crossed, 0.0), axis=1, keepdims=True)
         summed = jnp.where(small == g, part, summed)
-    res_out[...] = total + summed
+    scale_c = zero
+    for g in range(groups):
+        scale_c = jnp.where(small == g, scaled[g * modes : (g + 1) * modes], scale_c)
+    result = (total + summed) * scale_c * (1.0 / math.sqrt(float(rows * n * per)))
+    row = lax.broadcasted_iota(jnp.int32, (modes, chans), 0)
+    for g in range(groups):
+        first_col = jnp.broadcast_to(rolled(result, -g * per)[:, 0:1], (modes, chans))
+        only = jnp.where(row == lanes((modes, chans)), first_col, 0.0)
+        res_out[g : g + 1, :] = jnp.sum(only, axis=0, keepdims=True)[:, :modes]
+    write(res_out, out_hbm)
     last.wait()
     gf[:, rows : rows + 8, :] = gfr[...] * has_next
     for i in range(3):
         grad_out[i, rows - B : rows, :] = adjoint(i, rows - B, B).astype(BF16)
+    write(grad_out.at[:, rows - B : rows], grad_hbm.at[:, rows - B : rows])
     for copy in sent:
         copy.wait_send()
+    for copy in writes:
+        copy.wait()
+
+
+def write_out(mixed, grads, res, mixed_hbm, grads_hbm, res_hbm, sems):
+    pairs = [(grads.at[i], grads_hbm.at[i]) for i in range(3)]
+    pairs += [(mixed, mixed_hbm), (res, res_hbm)]
+    copies = [pltpu.make_async_copy(a, b, sems.at[i]) for i, (a, b) in enumerate(pairs)]
+    for copy in copies:
+        copy.start()
+    for copy in copies:
+        copy.wait()
 
 
 def body(n, raw_streams, short_taps, decay_rate, residue, medium_filter, cotangent):
@@ -359,25 +405,26 @@
     per = chans // groups
     raw = jnp.transpose(raw_streams, (1, 0, 2))
     taps = jnp.transpose(short_taps, (1, 0, 2))
-    scaled = jnp.sqrt(-jnp.expm1(-2.0 * decay_rate))
-    rhat = residue * scaled
-    rev = jnp.pad(medium_filter[:, ::-1], ((0, 0), (1, B - 1)))
     vm = pltpu.VMEM
     dma = pltpu.SemaphoreType.DMA
     hbm = pl.BlockSpec(memory_space=pltpu.HBM)
-    spec = pl.BlockSpec(memory_space=pltpu.VMEM)
+    shapes = (
+        jax.ShapeDtypeStruct((rows, chans), BF16),
+        jax.ShapeDtypeStruct((3, rows, chans), BF16),
+        jax.ShapeDtypeStruct((groups, modes), F32),
+    )
     mixed, grads, res = pl.pallas_call(
         functools.partial(kernel, n, groups, modes),
-        out_shape=(
-            jax.ShapeDtypeStruct((rows, chans), BF16),
-            jax.ShapeDtypeStruct((3, rows, chans), BF16),
-            jax.ShapeDtypeStruct((modes, chans), F32),
-        ),
-        in_specs=[hbm, spec, hbm, spec, spec, spec, spec],
-        out_specs=(spec, spec, spec),
+        out_shape=shapes,
+        in_specs=[hbm] * 6,
+        out_specs=(hbm, hbm, hbm),
         scratch_shapes=[
+            vm((rows, chans), BF16), vm((3, rows, chans), BF16), vm((groups, modes), F32),
+            dma((6,)),
+            vm(taps.shape, F32), vm(decay_rate.shape, F32), vm(residue.shape, F32),
+            vm(medium_filter.shape, F32),
             vm((3, rows, chans), BF16), vm((rows, chans), BF16),
-            vm((groups, 2 * B, 2 * B), BF16), vm((groups, 2 * B, 2 * B), BF16), dma((4,)),
+            vm((groups, 2 * B, 2 * B), BF16), vm((groups, 2 * B, 2 * B), BF16), dma((8,)),
             vm((2, 144, chans), BF16), vm((1, 16, chans), BF16),
             vm((1, B, chans), BF16), vm((B, chans), BF16),
             vm((3, rows + 8, chans), F32), vm((3, rows, chans), F32),
@@ -392,11 +439,18 @@
             dma((4,)), dma((4,)), dma((n,)), dma((n,)), dma((n,)), dma((n,)), dma, dma,
         ],
         compiler_params=pltpu.CompilerParams(
-            collective_id=0, has_side_effects=True, vmem_limit_bytes=48 * 2**20
+            collective_id=0, has_side_effects=True, vmem_limit_bytes=VMEM_LIMIT
         ),
-    )(raw, taps, cotangent, decay_rate, rhat, rev, medium_filter)
-    grad_residue = res[:, ::per].T * scaled / math.sqrt(float(rows * n * per))
-    return mixed, jnp.transpose(grads, (1, 0, 2)), grad_residue
+    )(raw, taps, cotangent, decay_rate, residue, medium_filter)
+    mixed, grads, res = pl.pallas_call(
+        write_out,
+        out_shape=shapes,
+        in_specs=[hbm] * 3,
+        out_specs=(hbm, hbm, hbm),
+        scratch_shapes=[dma((5,))],
+        compiler_params=pltpu.CompilerParams(has_side_effects=True, vmem_limit_bytes=VMEM_LIMIT),
+    )(mixed, grads, res)
+    return mixed, jnp.transpose(grads, (1, 0, 2)), res
 
 
 def solution(mesh):

time: 28.8 us -> 56.6 us (1.97)
  Pallas kernels: 21.9 us -> 55.8 us
  local copies, waits for them, and re-layouts: 4.55 us -> 0 us
  other arithmetic: 1.34 us -> 0 us
    pallas_call x1 -> x2, Pallas kernels: 21.9 us -> 55.8 us  [the longest x1 33 us: body(): pl.pallas_call(write_out, out_shape=shapes, in_specs=[hbm] * 3, out_specs...]
    unnamed x12 -> x0, local copies, waits for them, and re-layouts: 4.28 us -> none
    mul x1 -> x0, other arithmetic: 0.72 us -> none  [body(): rhat = residue * scaled]
    div x1 -> x0, other arithmetic: 0.62 us -> none  [body(): grad_residue = res[:, ::per].T * scaled / math.sqrt(float(rows * n * per))]
where the time goes in v3:
time: 56.6 us; the launch traced here: 56.5 us
  Pallas kernels  55.8 us (99%)
  between operations  0.64 us (1%)
    pallas_call x1, Pallas kernels, body(): pl.pallas_call(write_out, out_shape=shapes, in_specs=[hbm] * 3, out_specs...  33 us
    pallas_call x1, Pallas kernels, body(): pl.pallas_call(functools.partial(kernel, n, groups, modes), out_shape=sha...  22.8 us

profile of v3, /device:TPU:0, one launch (start us, length us, event | category | flops | bytes accessed | tf_op | source)
XLA Modules:
  0.0 56.5 jit_solution(7398617656747921586)
XLA Ops:
  0.6 22.8 %shard_map.85 = (bf16[1024,128]{1,0:T(8,128)(2,1)}, bf16[3,1024,128]{2,1,0:T(8,128)(2,1)}, f32[8,16]{1,0:T(8,128)}) custom-call(bf16[3,1024,128]{2,1,0:T(8,128)(2,1)} %bitcast.3, f32[3,7,128]{2,1,0:T(8,128)} %bitcast.4, bf16[1024,128]{1,0:T(8,128)(2,1)} %cot_hbm.1, f32[8,16]{1,0:T(8,128)} %rate_hbm.1, f32[8,16]{1,0:T(8,128)} %res_hbm.1, f32[8,128]{1,0:T(8,128)} %med_hbm.1), custom_call_target="tpu_custom_call" | custom-call | tf_op jit(solution)/shard_map/pallas_call | solution.py:416
  23.4 33.0 %shard_map.86 = (bf16[1024,128]{1,0:T(8,128)(2,1)}, bf16[3,1024,128]{2,1,0:T(8,128)(2,1)}, f32[8,16]{1,0:T(8,128)}) custom-call(bf16[1024,128]{1,0:T(8,128)(2,1)} %get-tuple-element.9.mixed, bf16[3,1024,128]{2,1,0:T(8,128)(2,1)} %get-tuple-element.10.grads, f32[8,16]{1,0:T(8,128)} %get-tuple-element.11.res), custom_call_target="tpu_custom_call" | custom-call | tf_op jit(solution)/shard_map/pallas_call | solution.py:445

commit v4 on v3

--- a/solution.py
+++ b/solution.py
@@ -389,13 +389,17 @@
         copy.wait()
 
 
-def write_out(mixed, grads, res, mixed_hbm, grads_hbm, res_hbm, sems):
-    pairs = [(grads.at[i], grads_hbm.at[i]) for i in range(3)]
-    pairs += [(mixed, mixed_hbm), (res, res_hbm)]
-    copies = [pltpu.make_async_copy(a, b, sems.at[i]) for i, (a, b) in enumerate(pairs)]
-    for copy in copies:
+def write_out(mixed, grads, res, mixed_hbm, grads_hbm, res_hbm, m_buf, g_buf, r_buf, ins, outs):
+    trips = [(grads.at[i], g_buf.at[i], grads_hbm.at[i]) for i in range(3)]
+    trips += [(mixed, m_buf, mixed_hbm), (res, r_buf, res_hbm)]
+    reads = [pltpu.make_async_copy(a, b, ins.at[i]) for i, (a, b, c) in enumerate(trips)]
+    stores = [pltpu.make_async_copy(b, c, outs.at[i]) for i, (a, b, c) in enumerate(trips)]
+    for copy in reads:
         copy.start()
-    for copy in copies:
+    for read, store in zip(reads, stores):
+        read.wait()
+        store.start()
+    for copy in stores:
         copy.wait()
 
 
@@ -447,7 +451,10 @@
         out_shape=shapes,
         in_specs=[hbm] * 3,
         out_specs=(hbm, hbm, hbm),
-        scratch_shapes=[dma((5,))],
+        scratch_shapes=[
+            vm((rows, chans), BF16), vm((3, rows, chans), BF16), vm((groups, modes), F32),
+            dma((5,)), dma((5,)),
+        ],
         compiler_params=pltpu.CompilerParams(has_side_effects=True, vmem_limit_bytes=VMEM_LIMIT),
     )(mixed, grads, res)
     return mixed, jnp.transpose(grads, (1, 0, 2)), res

time: 56.6 us -> 25.6 us (0.45)
  Pallas kernels: 55.8 us -> 24.8 us
    pallas_call x1, Pallas kernels: 33 us -> 2 us  [body(): pl.pallas_call(write_out, out_shape=shapes, in_specs=[hbm] * 3, out_specs...]
where the time goes in v4:
time: 25.6 us; the launch traced here: 25.4 us
  Pallas kernels  24.8 us (97%)
  between operations  0.64 us (2%)
    pallas_call x1, Pallas kernels, body(): pl.pallas_call(functools.partial(kernel, n, groups, modes), out_shape=sha...  22.8 us
    pallas_call x1, Pallas kernels, body(): pl.pallas_call(write_out, out_shape=shapes, in_specs=[hbm] * 3, out_specs...  2 us

profile of v4, /device:TPU:0, one launch (start us, length us, event | category | flops | bytes accessed | tf_op | source)
XLA Modules:
  0.0 25.4 jit_solution(2979675464959475490)
XLA Ops:
  0.6 22.8 %shard_map.85 = (bf16[1024,128]{1,0:T(8,128)(2,1)}, bf16[3,1024,128]{2,1,0:T(8,128)(2,1)}, f32[8,16]{1,0:T(8,128)}) custom-call(bf16[3,1024,128]{2,1,0:T(8,128)(2,1)} %bitcast.3, f32[3,7,128]{2,1,0:T(8,128)} %bitcast.4, bf16[1024,128]{1,0:T(8,128)(2,1)} %cot_hbm.1, f32[8,16]{1,0:T(8,128)} %rate_hbm.1, f32[8,16]{1,0:T(8,128)} %res_hbm.1, f32[8,128]{1,0:T(8,128)} %med_hbm.1), custom_call_target="tpu_custom_call" | custom-call | tf_op jit(solution)/shard_map/pallas_call | solution.py:420
  23.4 2.0 %shard_map.86 = (bf16[1024,128]{1,0:T(8,128)(2,1)}, bf16[3,1024,128]{2,1,0:T(8,128)(2,1)}, f32[8,16]{1,0:T(8,128)}) custom-call(bf16[1024,128]{1,0:T(8,128)(2,1)} %get-tuple-element.9.mixed, bf16[3,1024,128]{2,1,0:T(8,128)(2,1)} %get-tuple-element.10.grads, f32[8,16]{1,0:T(8,128)} %get-tuple-element.11.res), custom_call_target="tpu_custom_call" | custom-call | tf_op jit(solution)/shard_map/pallas_call | solution.py:449

commit v5 on v3

--- a/solution.py
+++ b/solution.py
@@ -12,7 +12,7 @@
 BF16 = jnp.bfloat16
 MESH = pl.DeviceIdType.MESH
 B = 128
-VMEM_LIMIT = 63 * 2**20
+VMEM_LIMIT = 64 * 2**20 - 1052672 - 131072
 
 
 def halves(x):
@@ -62,8 +62,7 @@
 def kernel(
     n, groups, modes,
     raw_hbm, taps_hbm, cot_hbm, rate_hbm, res_hbm, med_hbm,
-    mixed_hbm, grad_hbm, out_hbm,
-    mixed_out, grad_out, res_out, ws, taps, rate_ref, residue_ref, med_ref, raw, cot, tf, tb, ls,
+    mixed_out, grad_out, res_out, taps, rate_ref, residue_ref, med_ref, raw, cot, tf, tb, ls,
     hkv, hq, nq, ncot, ext, feat, hext, qext, yp, yg, head, tail,
     s_all, u_all, msg1, msg2, got1, got2, of, ob, gf, gfr,
     hs, hr, m1s, m1r, m2s, m2r, gs, gr,
@@ -334,16 +333,7 @@
         return 0
 
     lax.fori_loop(0, B // sub, from_groups, 0, unroll=B // sub)
-    writes = []
-
-    def write(src, dst):
-        copy = pltpu.make_async_copy(src, dst, ws.at[len(writes)])
-        copy.start()
-        writes.append(copy)
-
     last = send(gf.at[:, 0:8], gfr, gs, gr, prv)
-
-    write(mixed_out, mixed_hbm)
 
     def adjoint(i, start, size):
         total = tap[i][0] * gf[i, start : start + size, :]
@@ -354,7 +344,6 @@
     for i in range(3):
         for j in range(count - 1):
             grad_out[i, j * B : (j + 1) * B, :] = adjoint(i, j * B, B).astype(BF16)
-    write(grad_out.at[:, 0 : rows - B], grad_hbm.at[:, 0 : rows - B])
     for k in range(1, n):
         peer = lax.rem(me + k, n)
         pltpu.make_async_remote_copy(
@@ -377,25 +366,21 @@
         first_col = jnp.broadcast_to(rolled(result, -g * per)[:, 0:1], (modes, chans))
         only = jnp.where(row == lanes((modes, chans)), first_col, 0.0)
         res_out[g : g + 1, :] = jnp.sum(only, axis=0, keepdims=True)[:, :modes]
-    write(res_out, out_hbm)
     last.wait()
     gf[:, rows : rows + 8, :] = gfr[...] * has_next
     for i in range(3):
         grad_out[i, rows - B : rows, :] = adjoint(i, rows - B, B).astype(BF16)
-    write(grad_out.at[:, rows - B : rows], grad_hbm.at[:, rows - B : rows])
     for copy in sent:
         copy.wait_send()
-    for copy in writes:
-        copy.wait()
-
-
-def write_out(mixed, grads, res, mixed_hbm, grads_hbm, res_hbm, sems):
-    pairs = [(grads.at[i], grads_hbm.at[i]) for i in range(3)]
-    pairs += [(mixed, mixed_hbm), (res, res_hbm)]
-    copies = [pltpu.make_async_copy(a, b, sems.at[i]) for i, (a, b) in enumerate(pairs)]
-    for copy in copies:
+
+
+def write_out(mixed, grads, res, mixed_hbm, grads_hbm, res_hbm, outs):
+    trips = [(grads.at[i], grads_hbm.at[i]) for i in range(3)]
+    trips += [(mixed, mixed_hbm), (res, res_hbm)]
+    stores = [pltpu.make_async_copy(a, b, outs.at[i]) for i, (a, b) in enumerate(trips)]
+    for copy in stores:
         copy.start()
-    for copy in copies:
+    for copy in stores:
         copy.wait()
 
 
@@ -407,6 +392,7 @@
     taps = jnp.transpose(short_taps, (1, 0, 2))
     vm = pltpu.VMEM
     dma = pltpu.SemaphoreType.DMA
+    spec = pl.BlockSpec(memory_space=pltpu.VMEM)
     hbm = pl.BlockSpec(memory_space=pltpu.HBM)
     shapes = (
         jax.ShapeDtypeStruct((rows, chans), BF16),
@@ -415,12 +401,10 @@
     )
     mixed, grads, res = pl.pallas_call(
         functools.partial(kernel, n, groups, modes),
-        out_shape=shapes,
+        out_shape=tuple(pltpu.VMEM(x.shape, x.dtype) for x in shapes),
         in_specs=[hbm] * 6,
-        out_specs=(hbm, hbm, hbm),
+        out_specs=(spec, spec, spec),
         scratch_shapes=[
-            vm((rows, chans), BF16), vm((3, rows, chans), BF16), vm((groups, modes), F32),
-            dma((6,)),
             vm(taps.shape, F32), vm(decay_rate.shape, F32), vm(residue.shape, F32),
             vm(medium_filter.shape, F32),
             vm((3, rows, chans), BF16), vm((rows, chans), BF16),
@@ -445,10 +429,12 @@
     mixed, grads, res = pl.pallas_call(
         write_out,
         out_shape=shapes,
-        in_specs=[hbm] * 3,
+        in_specs=[spec] * 3,
         out_specs=(hbm, hbm, hbm),
-        scratch_shapes=[dma((5,))],
-        compiler_params=pltpu.CompilerParams(has_side_effects=True, vmem_limit_bytes=VMEM_LIMIT),
+        scratch_shapes=[
+            dma((5,)),
+        ],
+        compiler_params=pltpu.CompilerParams(has_side_effects=True, vmem_limit_bytes=2**20),
     )(mixed, grads, res)
     return mixed, jnp.transpose(grads, (1, 0, 2)), res
 

time: 56.6 us -> 23.9 us (0.42)
  Pallas kernels: 55.8 us -> 23.1 us
    pallas_call x2, Pallas kernels: 55.8 us -> 23.1 us  [the longest x1 22.1 us: body(): pl.pallas_call(functools.partial(kernel, n, groups, modes), out_shape=tup...]
where the time goes in v5:
time: 23.9 us; the launch traced here: 23.8 us
  Pallas kernels  23.1 us (97%)
  between operations  0.64 us (3%)
    pallas_call x1, Pallas kernels, body(): pl.pallas_call(functools.partial(kernel, n, groups, modes), out_shape=tup...  22.1 us
    pallas_call x1, Pallas kernels, body(): pl.pallas_call(write_out, out_shape=shapes, in_specs=[spec] * 3, out_spec...  1.01 us

profile of v5, /device:TPU:0, one launch (start us, length us, event | category | flops | bytes accessed | tf_op | source)
XLA Modules:
  0.0 23.8 jit_solution(6600061946806350348)
XLA Ops:
  0.6 22.1 %shard_map.85 = (bf16[1024,128]{1,0:T(8,128)(2,1)S(1)}, bf16[3,1024,128]{2,1,0:T(8,128)(2,1)S(1)}, f32[8,16]{1,0:T(8,128)S(1)}) custom-call(bf16[3,1024,128]{2,1,0:T(8,128)(2,1)} %bitcast.3, f32[3,7,128]{2,1,0:T(8,128)} %bitcast.4, bf16[1024,128]{1,0:T(8,128)(2,1)} %cot_hbm.1, f32[8,16]{1,0:T(8,128)} %rate_hbm.1, f32[8,16]{1,0:T(8,128)} %res_hbm.1, ...), custom_call_target="tpu_custom_call" | custom-call | tf_op jit(solution)/shard_map/pallas_call | solution.py:402
  22.8 1.0 %shard_map.86 = (bf16[1024,128]{1,0:T(8,128)(2,1)}, bf16[3,1024,128]{2,1,0:T(8,128)(2,1)}, f32[8,16]{1,0:T(8,128)}) custom-call(bf16[1024,128]{1,0:T(8,128)(2,1)S(1)} %get-tuple-element.9.mixed, bf16[3,1024,128]{2,1,0:T(8,128)(2,1)S(1)} %get-tuple-element.10.grads, f32[8,16]{1,0:T(8,128)S(1)} %get-tuple-element.11.res), custom_call_target="tpu_custom_call" | custom-call | tf_op jit(solution)/shard_map/pallas_call | solution.py:429

commit v6 on v5

--- a/solution.py
+++ b/solution.py
@@ -320,20 +320,24 @@
         of[g] = of[g] + carried(e1t, starts, g)
         ob[g] = ob[g] + carried(e2t, ends, g)
 
+    def aligned(start):
+        return pl.ds(start if isinstance(start, int) else pl.multiple_of(start, sub), sub)
+
     def from_groups(t, _):
-        there = pl.ds(pl.multiple_of(t * sub, sub), sub)
+        there = aligned(t * sub)
         mixed = block_transpose([of[g, there, :] for g in range(groups)], per)
         grads = block_transpose([ob[g, there, :] for g in range(groups)], per)
         for j in range(count):
-            here = pl.ds(pl.multiple_of(j * B + t * sub, sub), sub)
+            here = aligned(j * B + t * sub)
             mixed_out[here, :] = (feat[0, here, :] * mixed[j]).astype(BF16)
             gf[0, here, :] = cot[here, :].astype(F32) * mixed[j]
             gf[1, here, :] = grads[j] * feat[2, here, :]
             gf[2, here, :] = grads[j] * feat[1, here, :]
         return 0
 
-    lax.fori_loop(0, B // sub, from_groups, 0, unroll=B // sub)
+    from_groups(0, 0)
     last = send(gf.at[:, 0:8], gfr, gs, gr, prv)
+    lax.fori_loop(1, B // sub, from_groups, 0, unroll=B // sub - 1)
 
     def adjoint(i, start, size):
         total = tap[i][0] * gf[i, start : start + size, :]

time: 23.9 us -> 23.7 us (level)
  no operation moved by 1% of the time
where the time goes in v6:
time: 23.7 us; the launch traced here: 23.6 us
  Pallas kernels  22.9 us (97%)
  between operations  0.64 us (3%)
    pallas_call x1, Pallas kernels, body(): pl.pallas_call(functools.partial(kernel, n, groups, modes), out_shape=tup...  21.9 us
    pallas_call x1, Pallas kernels, body(): pl.pallas_call(write_out, out_shape=shapes, in_specs=[spec] * 3, out_spec...  1.01 us

profile of v6, /device:TPU:0, one launch (start us, length us, event | category | flops | bytes accessed | tf_op | source)
XLA Modules:
  0.0 23.6 jit_solution(5323034179324188344)
XLA Ops:
  0.6 21.9 %shard_map.85 = (bf16[1024,128]{1,0:T(8,128)(2,1)S(1)}, bf16[3,1024,128]{2,1,0:T(8,128)(2,1)S(1)}, f32[8,16]{1,0:T(8,128)S(1)}) custom-call(bf16[3,1024,128]{2,1,0:T(8,128)(2,1)} %bitcast.3, f32[3,7,128]{2,1,0:T(8,128)} %bitcast.4, bf16[1024,128]{1,0:T(8,128)(2,1)} %cot_hbm.1, f32[8,16]{1,0:T(8,128)} %rate_hbm.1, f32[8,16]{1,0:T(8,128)} %res_hbm.1, ...), custom_call_target="tpu_custom_call" | custom-call | tf_op jit(solution)/shard_map/pallas_call | solution.py:406
  22.6 1.0 %shard_map.86 = (bf16[1024,128]{1,0:T(8,128)(2,1)}, bf16[3,1024,128]{2,1,0:T(8,128)(2,1)}, f32[8,16]{1,0:T(8,128)}) custom-call(bf16[1024,128]{1,0:T(8,128)(2,1)S(1)} %get-tuple-element.9.mixed, bf16[3,1024,128]{2,1,0:T(8,128)(2,1)S(1)} %get-tuple-element.10.grads, f32[8,16]{1,0:T(8,128)S(1)} %get-tuple-element.11.res), custom_call_target="tpu_custom_call" | custom-call | tf_op jit(solution)/shard_map/pallas_call | solution.py:433
